TPU v7x, 32 devices: a whole 2x2x4 slice. The times are simulated.
32 devices in a mesh: grp: 2 (over y), chan: 8 (over z, x), band: 2 (over core).
Axes of the slice: x: 2, y: 2, z: 4, core: 2. Of those that a mesh axis runs over, the one named last changes fastest.
Arguments:
- spectra: float32 [2, 32, 1280, 256], P(None, 'band', ('grp', 'chan')), parts along dimension 2, may hold values from -6 to 6
- channel_order: int32 [16, 80], P(('grp', 'chan')), parts along dimension 0, may hold values from 0 to 79, each once within a row
- bin_assign: int32 [32], replicated, may hold values from 0 to 31, each once
Outputs:
- correlations: float32 [16, 3, 64, 6400], P(('grp', 'chan'), None, None, 'band'), parts along dimension 0
There are 2 independent parts, one for each index of `grp`. A program takes and returns all parts, laid end to end along the dimension named above; an argument that names none is the same for every part. Nothing has to cross between parts.
Inputs may be any that keep to these rules, and one draw needn't show every extreme that they name: `channel_order`: each row is a permutation of 0 .. 79. `bin_assign`: a permutation of 0 .. 31.
All inputs are finite; a program needn't handle non-finite values.
Results may differ from a plain program's by a relative error of at most 0.0003.
Values sent between devices are 32-bit elements; how exact they have to be, the bound alone decides.
A program may use at most 128 MiB of HBM per device.

v0:
```python
import math

import jax
import jax.numpy as jnp
from jax import lax
from jax.sharding import PartitionSpec as P

HIGHEST = lax.Precision.HIGHEST


def shifted(block, axis, distance):
    devices = range(lax.axis_size(axis))
    route = [((i - distance) % len(devices), i) for i in devices]
    return lax.ppermute(block, axis, route)


def cross_spectra(first_block, second_block, factor):
    left_real = jnp.concatenate([first_block[0], first_block[1]], axis=2)
    left_imag = jnp.concatenate([first_block[1], -first_block[0]], axis=2)
    left_both = jnp.stack([left_real, left_imag])
    right_both = jnp.concatenate([second_block[0], second_block[1]], axis=2)
    products = jnp.einsum("rfiw,fjw->rfij", left_both, right_both, precision=HIGHEST)
    bins_here = first_block.shape[1]
    row_count = first_block.shape[2]
    return products.reshape(2, bins_here, row_count * row_count) * factor


def lag_table(bin_assign, lag_count):
    lag_steps = jnp.arange(lag_count, dtype=jnp.int32)
    phase_step = lag_steps[:, None] * bin_assign[None, :] % lag_count
    angles = phase_step.astype(jnp.float32) * (2.0 * math.pi / lag_count)
    return jnp.stack([jnp.cos(angles), -jnp.sin(angles)], axis=1)


def on_device(spectra, channel_order, bin_assign):
    local_block = spectra[:, :, channel_order[0], :]
    window_count = spectra.shape[3]
    factor = 1.0 / window_count
    loop_size = lax.axis_size("chan")
    quarter_loop = loop_size // 4
    half_loop = loop_size // 2
    near_block = shifted(local_block, "chan", -quarter_loop)
    same_pair = cross_spectra(local_block, local_block, factor)
    near_pair = cross_spectra(local_block, near_block, factor)
    far_block = shifted(local_block, "chan", -half_loop)
    far_pair = cross_spectra(local_block, far_block, factor)
    stacked = jnp.stack([same_pair, near_pair, far_pair])
    lag_weights = lag_table(bin_assign, 2 * bin_assign.shape[0])
    result = jnp.einsum(
        "lrs,prsc->plc",
        lag_weights,
        lax.all_to_all(stacked, "band", split_axis=3, concat_axis=2, tiled=True),
        precision=HIGHEST,
    )
    return result[None]


def solution(mesh):
    in_specs = (P(None, "band", ("grp", "chan"), None), P(("grp", "chan"), None), P())
    out_specs = P(("grp", "chan"), None, None, "band")
    return jax.shard_map(
        on_device, mesh=mesh, in_specs=in_specs, out_specs=out_specs, check_vma=False
    )
```

profile of v0, /device:TPU:0, one launch (start us, length us, event | category | flops | bytes accessed | tf_op | source)
XLA Modules:
  0.0 338.3 jit_solution(12644584561572352009)
XLA Ops:
  0.0 0.0 copy-start
  0.0 0.8 fusion.20
  0.8 0.9 copy-done
  1.8 7.9 %gather_fusion = f32[80,2,16,256]{3,0,2,1:T(8,128)} fusion(f32[2,16,80,256]{3,2,1,0:T(8,128)S(1)} %copy-done, s32[1024]{0:T(1024)S(1)} %pad_clamp_fusion), kind=kCustom, calls=%fused_computation | custom fusion | bytes 5243200 | tf_op jit(solution)/shard_map/gather | solution.py:36
  9.7 0.0 copy-start.5
  9.7 5.5 %collective-permute-start = (f32[2,16,80,256]{3,2,1,0:T(8,128)}, f32[2,16,80,256]{3,2,1,0:T(8,128)}, u32[]{:S(2)}, u32[]{:S(2)}) collective-permute-start(f32[2,16,80,256]{3,2,1,0:T(8,128)} %bitcast.78), channel_id=1, source_target_pairs={{4,0},{6,2},{8,4},{10,6},{12,8},{14,10},{0,12},{2,14},{5,1},{7,3},... | collective-permute-start | bytes 7864328 | tf_op jit(solution)/shard_map/ppermute | solution.py:14
  15.2 0.0 collective-permute-start.1
  15.2 1.5 fusion.25
  16.7 0.0 copy-done.5
  16.7 0.2 slice_bitcast_fusion.5
  16.9 0.4 fusion.8
  17.3 0.0 copy-start.2
  17.3 1.5 copy-done.2
  18.8 8.0 %multiply_bitcast_fusion.2 = f32[2,16,80,80]{2,3,0,1:T(8,128)} fusion(f32[1,16,80,512]{3,2,0,1:T(8,128)S(1)} %get-tuple-element.12, f32[1,16,80,512]{3,2,0,1:T(8,128)S(1)} %get-tuple-element.11, f32[16,80,256]{2,1,0:T(8,128)S(1)} %get-tuple-element.10, f32[16,80,256]{2,1,0:T(8,128)S(1)} %get-tuple-element.9), kind=kOutput, calls=%fused_computation.25 | convolution fusion | flops 1260462080 | bytes 8683520 | tf_op jit(solution)/shard_map/rfiw,fjw->rfij/dot_general | solution.py:22
  26.7 0.0 copy-start.6
  26.7 2.8 copy.11
  29.6 1.8 mul.91
  31.4 0.0 copy-done.6
  31.4 0.2 fusion.19
  31.6 0.0 copy-start.3
  31.6 41.2 %collective-permute-done = f32[2,16,80,256]{3,2,1,0:T(8,128)} collective-permute-done((f32[2,16,80,256]{3,2,1,0:T(8,128)}, f32[2,16,80,256]{3,2,1,0:T(8,128)}, u32[]{:S(2)}, u32[]{:S(2)}) %collective-permute-start) | collective-permute-done | bytes 2621472 | tf_op jit(solution)/shard_map/ppermute | solution.py:14
  72.8 1.9 slice_bitcast_fusion.3
  74.7 0.0 copy-done.3
  74.7 8.1 %multiply_bitcast_fusion.1 = f32[2,16,80,80]{2,3,0,1:T(8,128)} fusion(f32[1,16,80,512]{3,2,0,1:T(8,128)S(1)} %copy-done.3, f32[1,16,80,512]{3,2,0,1:T(8,128)S(1)} %get-tuple-element.11, f32[16,80,256]{2,1,0:T(8,128)S(1)} %get-tuple-element.6, f32[16,80,256]{2,1,0:T(8,128)S(1)} %get-tuple-element.5), kind=kOutput, calls=%fused_computation.24 | convolution fusion | flops 1260462080 | bytes 8683520 | tf_op jit(solution)/shard_map/rfiw,fjw->rfij/dot_general | solution.py:22
  82.8 2.9 copy.12
  85.7 2.7 mul.94
  88.4 0.0 copy-start.4
  88.4 95.5 %collective-permute-done.1 = f32[2,16,80,256]{3,2,1,0:T(8,128)} collective-permute-done((f32[2,16,80,256]{3,2,1,0:T(8,128)}, f32[2,16,80,256]{3,2,1,0:T(8,128)}, u32[]{:S(2)}, u32[]{:S(2)}) %collective-permute-start.1) | collective-permute-done | bytes 2621472 | tf_op jit(solution)/shard_map/ppermute | solution.py:14
  183.9 1.9 slice_bitcast_fusion.1
  185.8 0.0 copy-done.4
  185.8 8.0 %multiply_bitcast_fusion = f32[2,16,80,80]{2,3,0,1:T(8,128)} fusion(f32[1,16,80,512]{3,2,0,1:T(8,128)S(1)} %copy-done.4, f32[1,16,80,512]{3,2,0,1:T(8,128)S(1)} %get-tuple-element.11, f32[16,80,256]{2,1,0:T(8,128)S(1)} %get-tuple-element.8, f32[16,80,256]{2,1,0:T(8,128)S(1)} %get-tuple-element.7), kind=kOutput, calls=%fused_computation.23 | convolution fusion | flops 1260462080 | bytes 8683520 | tf_op jit(solution)/shard_map/rfiw,fjw->rfij/dot_general | solution.py:22
  193.8 1.7 copy.13
  195.5 1.4 mul.97
  196.9 1.6 pad_maximum_fusion.5
  198.5 17.6 %copy.14 = f32[3,2,16,6400]{2,1,0,3:T(2,128)} copy(f32[3,2,16,6400]{3,2,1,0:T(8,128)S(1)} %pad_maximum_fusion.5) | data formatting | bytes 4915200 | tf_op jit(solution)/shard_map/stack | solution.py:47
  216.0 38.7 %reshape.174 = f32[2,1,307200]{2,1,0:T(1,128)} reshape(f32[6400,3,2,16]{3,2,1,0:T(2,128)} %bitcast.76) | data formatting | bytes 4915200
  254.7 6.9 %all_to_all.18 = f32[2,1,307200]{2,1,0:T(1,128)S(1)} all-to-all(f32[2,1,307200]{2,1,0:T(1,128)} %reshape.174), channel_id=1, replica_groups=mesh['grp'=2,'chan'=8,'band'=2] {'band'}, dimensions={0} | all-to-all | bytes 4915200 | tf_op jit(solution)/shard_map/all_to_all | solution.py:52
  261.6 0.6 broadcast.163
  262.2 9.7 %reduce = f32[2,307200]{1,0:T(2,128)} reduce(f32[2,1,307200]{2,1,0:T(1,128)S(1)} %all_to_all.18, f32[]{:T(128)} %broadcast.163), dimensions={1}, to_apply=%all_to_all.13.reduce_sub_computation | reduce | bytes 4915204 | tf_op jit(solution)/shard_map/all_to_all | solution.py:52
  271.9 39.0 %reshape.175 = f32[6400,3,2,16]{3,2,1,0:T(2,128)} reshape(f32[2,307200]{1,0:T(2,128)} %reduce) | data formatting | bytes 4915200
  310.9 21.8 %copy.16 = f32[3,2,2,16,3200]{4,3,2,1,0:T(8,128)} copy(f32[3,2,2,16,3200]{3,1,0,4,2:T(2,128)} %bitcast.77) | data formatting | bytes 4915200 | tf_op jit(solution)/shard_map/all_to_all | solution.py:52
  332.7 0.0 copy-start.1
  332.7 5.5 %convolution_bitcast_fusion = f32[1,3,64,3200]{3,2,1,0:T(8,128)} fusion(f32[3,2,32,3200]{3,2,1,0:T(8,128)} %bitcast.82, f32[64,1,32]{0,2,1:T(8,128)S(1)} %get-tuple-element.14, f32[64,1,32]{0,2,1:T(8,128)S(1)} %get-tuple-element.13), kind=kOutput, calls=%fused_computation.2 | convolution fusion | flops 471863296 | bytes 4931584 | tf_op jit(solution)/shard_map/lrs,prsc->plc/dot_general | solution.py:49
  338.2 0.0 copy-done.1
  (1 shorter events, 0.0 us)
Async XLA Ops:
  0.0 1.8 copy-start
  9.7 7.0 %copy-start.5 = (f32[80,2,16,256]{3,0,2,1:T(8,128)S(1)}, f32[80,2,16,256]{3,0,2,1:T(8,128)}, u32[]{:S(2)}) copy-start(f32[80,2,16,256]{3,0,2,1:T(8,128)} %gather_fusion) | copy-start | bytes 7864324
  9.7 63.1 %collective-permute-start = (f32[2,16,80,256]{3,2,1,0:T(8,128)}, f32[2,16,80,256]{3,2,1,0:T(8,128)}, u32[]{:S(2)}, u32[]{:S(2)}) collective-permute-start(f32[2,16,80,256]{3,2,1,0:T(8,128)} %bitcast.78), channel_id=1, source_target_pairs={{4,0},{6,2},{8,4},{10,6},{12,8},{14,10},{0,12},{2,14},{5,1},{7,3},... | collective-permute-start | bytes 7864328 | tf_op jit(solution)/shard_map/ppermute | solution.py:14
  15.2 168.7 %collective-permute-start.1 = (f32[2,16,80,256]{3,2,1,0:T(8,128)}, f32[2,16,80,256]{3,2,1,0:T(8,128)}, u32[]{:S(2)}, u32[]{:S(2)}) collective-permute-start(f32[2,16,80,256]{3,2,1,0:T(8,128)} %bitcast.79), channel_id=1, source_target_pairs={{8,0},{10,2},{12,4},{14,6},{0,8},{2,10},{4,12},{6,14},{9,1},{11,3}... | collective-permute-start | bytes 7864328 | tf_op jit(solution)/shard_map/ppermute | solution.py:14
  17.3 1.5 copy-start.2
  26.7 4.6 %copy-start.6 = (s32[32]{0:T(128)S(1)}, s32[32]{0:T(128)}, u32[]{:S(2)}) copy-start(s32[32]{0:T(128)} %param.5) | copy-start | bytes 388
  31.6 43.1 %copy-start.3 = (f32[1,16,80,512]{3,2,0,1:T(8,128)S(1)}, f32[1,16,80,512]{3,2,0,1:T(8,128)}, u32[]{:S(2)}) copy-start(f32[1,16,80,512]{3,2,0,1:T(8,128)} %copy-done.2) | copy-start | bytes 7864324
  88.4 97.4 %copy-start.4 = (f32[1,16,80,512]{3,2,0,1:T(8,128)S(1)}, f32[1,16,80,512]{3,2,0,1:T(8,128)}, u32[]{:S(2)}) copy-start(f32[1,16,80,512]{3,2,0,1:T(8,128)} %copy-done.2) | copy-start | bytes 7864324
  332.7 5.5 %copy-start.1 = (f32[2,16,80,256]{3,2,1,0:T(8,128)S(1)}, f32[2,16,80,256]{3,2,1,0:T(8,128)}, u32[]{:S(2)}) copy-start(f32[2,16,80,256]{3,2,1,0:T(8,128)} %param.3) | copy-start | bytes 7864324
where the time goes:
time: 344 us; the launch traced here: 338 us
  local copies, waits for them, and re-layouts  145 us (42%)
  waiting for transfers between devices  137 us (40%)
  matrix products  29.5 us (9%)
  other arithmetic  14.2 us (4%)
  blocking collectives  6.94 us (2%)
  starting transfers between devices  5.49 us (2%)
    ppermute x2, waiting for transfers between devices, shifted(): return lax.ppermute(block, axis, route)  137 us
    unnamed x16, local copies, waits for them, and re-layouts  80.1 us
    dot_general x3, matrix products, cross_spectra(): jnp.einsum('rfiw,fjw->rfij', left_both, right_both, precision=HIGHEST)  24 us
    all_to_all x2, local copies, waits for them, and re-layouts, on_device(): lax.all_to_all(stacked, 'band', split_axis=3, concat_axis=2, tiled=True)  22.3 us
    another operation x1, local copies, waits for them, and re-layouts, on_device(): stacked = jnp.stack([same_pair, near_pair, far_pair])  17.6 us
    mul x6, local copies, waits for them, and re-layouts, cross_spectra(): return products.reshape(2, bins_here, row_count * row_count) * factor  13.4 us
    all_to_all x1, other arithmetic, on_device(): lax.all_to_all(stacked, 'band', split_axis=3, concat_axis=2, tiled=True)  9.74 us
    gather x1, local copies, waits for them, and re-layouts, on_device(): local_block = spectra[:, :, channel_order[0], :]  7.93 us
  transfers between devices with their start and end apart: 2, of which 2 were waited for; matrix products, arithmetic and copies ran while one was open for 9% of the time, Pallas kernels for 0%

commit v1 on v0

v1 whole, which is shorter than its diff:
```python
import functools
import math

import jax
import jax.numpy as jnp
from jax import lax
from jax.experimental import pallas as pl
from jax.experimental.pallas import tpu as pltpu
from jax.sharding import PartitionSpec as P

MEMBERS = 4
F32 = jnp.float32
BF16 = jnp.bfloat16
VMEM = pl.BlockSpec(memory_space=pltpu.VMEM)
SMEM = pl.BlockSpec(memory_space=pltpu.SMEM)
LIMIT = 40 * 1024 * 1024


def halves(x):
    high = x.astype(BF16)
    low = (x - high.astype(F32)).astype(BF16)
    return high, low


def thirds(x):
    high = x.astype(BF16)
    rest = x - high.astype(F32)
    middle = rest.astype(BF16)
    low = (rest - middle.astype(F32)).astype(BF16)
    return high, middle, low


def dot(left, right, dims):
    return lax.dot_general(left, right, (dims, ((), ())), preferred_element_type=F32)


def order_kernel(distance, place, order, spectra, ordered):
    parts, bins, rows, _ = ordered.shape
    chunk = lax.rem(place[0] + distance, MEMBERS)
    row_ids = lax.broadcasted_iota(jnp.int32, (rows, rows), 0)
    chosen = jnp.where(row_ids == order[...], 1.0, 0.0).astype(BF16)
    chosen = jnp.concatenate([chosen] * 3, axis=0)
    for part in range(parts):
        for slot in range(bins):
            values = spectra[part, chunk * bins + slot]
            stacked = jnp.concatenate(thirds(values), axis=0)
            ordered[part, slot] = dot(chosen, stacked, ((0,), (0,)))


def ordered_chunk(place, order, spectra, distance):
    parts, bins, rows, windows = spectra.shape
    return pl.pallas_call(
        functools.partial(order_kernel, distance),
        out_shape=jax.ShapeDtypeStruct((parts, bins // MEMBERS, rows, windows), F32),
        in_specs=[SMEM, VMEM, VMEM],
        out_specs=VMEM,
        compiler_params=pltpu.CompilerParams(vmem_limit_bytes=LIMIT),
        name=f"order_{distance}",
    )(place, order, spectra)


def left_operand(real, imag):
    stacked = jnp.concatenate(
        [
            jnp.concatenate([real, imag], axis=1),
            jnp.concatenate([imag, -real], axis=1),
        ],
        axis=0,
    )
    return halves(stacked)


def right_operand(real, imag):
    return halves(jnp.concatenate([real, imag], axis=1))


def product(left, right):
    dims = ((1,), (1,))
    return (
        dot(left[0], right[0], dims)
        + dot(left[0], right[1], dims)
        + dot(left[1], right[0], dims)
    )


def packed_rows(scratch, lead, first, rows, group, count):
    pieces = [
        scratch[lead, pl.ds(first + group * 8 + step, count, stride=rows), :][:, :rows]
        for step in range(8)
    ]
    return jnp.concatenate(pieces, axis=1)


def self_kernel(place, *refs):
    chunks, (same, other), scratch = refs[:MEMBERS], refs[MEMBERS:-1], refs[-1]
    _, bins, rows, _ = chunks[0].shape
    half = rows // 2
    count = 2 * bins
    width = 8 * rows
    for distance in range(MEMBERS):
        chunk = chunks[distance]
        block = (MEMBERS - distance) % MEMBERS
        for slot in range(bins):
            real, imag = chunk[0, slot], chunk[1, slot]
            value = product(left_operand(real, imag), right_operand(real, imag))
            scratch[distance, slot * 2 * rows : (slot + 1) * 2 * rows, 0:rows] = value
        for out, shift in ((same, 0), (other, 1)):
            first = lax.rem(place[1] + shift, 2) * half
            for group in range(half // 8):
                out[block * count : (block + 1) * count, group * width : (group + 1) * width] = (
                    packed_rows(scratch, distance, first, rows, group, count)
                )


def pair_kernel(place, *refs):
    blocks, outs, scratch = refs[:MEMBERS], refs[MEMBERS:-1], refs[-1]
    _, bins, rows, _ = blocks[0].shape
    half = rows // 2
    count = 2 * bins
    width = 8 * rows
    for slot in range(bins):
        rights = []
        lefts = []
        for block in blocks:
            real, imag = block[0, slot], block[1, slot]
            rights.append(right_operand(real, imag))
            lefts.append(left_operand(real, imag))
        for owner in range(MEMBERS):
            for pair in range(2):
                partner = (owner + pair + 1) % MEMBERS
                scratch[owner * 2 + pair, slot * 2 * rows : (slot + 1) * 2 * rows, 0:rows] = (
                    product(lefts[owner], rights[partner])
                )
    for owner in range(MEMBERS):
        for shift in range(2):
            first = lax.rem(place[1] + shift, 2) * half
            for pair in range(2):
                for group in range(half // 8):
                    outs[owner * 2 + shift][pair, :, group * width : (group + 1) * width] = (
                        packed_rows(scratch, owner * 2 + pair, first, rows, group, count)
                    )


def self_pairs(place, chunks):
    _, bins, rows, windows = chunks[0].shape
    columns = rows * rows // 2
    shape = jax.ShapeDtypeStruct((MEMBERS * 2 * bins, columns), F32)
    flops = MEMBERS * bins * 3 * 2 * 4 * rows * rows * windows
    return pl.pallas_call(
        self_kernel,
        out_shape=(shape, shape),
        in_specs=[SMEM] + [VMEM] * MEMBERS,
        out_specs=(VMEM, VMEM),
        scratch_shapes=[pltpu.VMEM((MEMBERS, 2 * bins * rows, 128), F32)],
        compiler_params=pltpu.CompilerParams(vmem_limit_bytes=LIMIT),
        cost_estimate=pl.CostEstimate(flops=flops * 8, bytes_accessed=1 << 22, transcendentals=0),
        name="self_pairs",
    )(place, *chunks)


def partner_pairs(place, blocks):
    _, bins, rows, windows = blocks[0].shape
    columns = rows * rows // 2
    shape = jax.ShapeDtypeStruct((2, 2 * bins, columns), F32)
    flops = 2 * MEMBERS * bins * 3 * 2 * 4 * rows * rows * windows
    return pl.pallas_call(
        pair_kernel,
        out_shape=(shape,) * (2 * MEMBERS),
        in_specs=[SMEM] + [VMEM] * MEMBERS,
        out_specs=(VMEM,) * (2 * MEMBERS),
        scratch_shapes=[pltpu.VMEM((2 * MEMBERS, 2 * bins * rows, 128), F32)],
        compiler_params=pltpu.CompilerParams(vmem_limit_bytes=LIMIT),
        cost_estimate=pl.CostEstimate(flops=flops, bytes_accessed=1 << 22, transcendentals=0),
        name="partner_pairs",
    )(place, *blocks)


def lag_kernel(table, same, other, *refs):
    pieces, out = refs[:-1], refs[-1]
    columns = out.shape[2]
    tile = 640 if columns % 640 == 0 else columns
    high, low = halves(table[...])
    dims = ((1,), (0,))
    for pair in range(3):
        for at in range(0, columns, tile):
            span = slice(at, at + tile)
            if pair == 0:
                stacked = jnp.concatenate([same[:, span], other[:, span]], axis=0)
            else:
                stacked = jnp.concatenate([piece[pair - 1, :, span] for piece in pieces], axis=0)
            first, second = halves(stacked)
            out[pair, :, span] = dot(high, first, dims) + dot(high, second, dims) + dot(low, first, dims)


def lag_transform(table, same, other, pieces):
    lags = table.shape[0]
    columns = same.shape[1]
    return pl.pallas_call(
        lag_kernel,
        out_shape=jax.ShapeDtypeStruct((3, lags, columns), F32),
        in_specs=[VMEM] * (3 + len(pieces)),
        out_specs=VMEM,
        compiler_params=pltpu.CompilerParams(vmem_limit_bytes=LIMIT),
        name="lag_transform",
    )(table, same, other, *pieces)


def lag_table(bin_assign, member, band, factor):
    bins = bin_assign.shape[0]
    lags = 2 * bins
    chunk = bins // (2 * MEMBERS)
    column = jnp.arange(lags, dtype=jnp.int32)
    shift = column // (MEMBERS * 2 * chunk)
    distance = column // (2 * chunk) % MEMBERS
    slot = column // 2 % chunk
    part = column % 2
    where = (band + shift) % 2 * (MEMBERS * chunk) + (member - distance + MEMBERS) % MEMBERS * chunk + slot
    steps = jnp.arange(lags, dtype=jnp.int32)
    phase = steps[:, None] * bin_assign[where][None, :] % lags
    angles = phase.astype(F32) * (2.0 * math.pi / lags)
    return jnp.where(part[None, :] == 0, jnp.cos(angles), -jnp.sin(angles)) * factor


def on_device(loop_size, spectra, channel_order, bin_assign):
    quarter = loop_size // MEMBERS
    chan = lax.axis_index("chan")
    band = lax.axis_index("band")
    member = chan // quarter
    place = jnp.stack([member, band]).astype(jnp.int32)
    blocks = [None] * MEMBERS
    chunks = [None] * MEMBERS
    for distance in (2, 3, 1, 0):
        chunk = ordered_chunk(place, channel_order, spectra, distance)
        chunks[distance] = chunk
        if distance:
            route = [(i, (i + distance * quarter) % loop_size) for i in range(loop_size)]
            blocks[MEMBERS - distance] = lax.ppermute(chunk, "chan", route)
        else:
            blocks[0] = chunk
    same, other = self_pairs(place, chunks)
    other = lax.ppermute(other, "band", [(0, 1), (1, 0)])
    results = partner_pairs(place, blocks)
    pieces = []
    for shift in range(2):
        for distance in range(MEMBERS):
            piece = results[distance * 2 + shift]
            if distance or shift:
                route = [
                    (i * 2 + j, (i + distance * quarter) % loop_size * 2 + (j + shift) % 2)
                    for i in range(loop_size)
                    for j in range(2)
                ]
                piece = lax.ppermute(piece, ("chan", "band"), route)
            pieces.append(piece)
    table = lag_table(bin_assign, member, band, 1.0 / spectra.shape[3])
    return lag_transform(table, same, other, pieces)[None]


def solution(mesh):
    in_specs = (P(None, "band", ("grp", "chan"), None), P(("grp", "chan"), None), P())
    out_specs = P(("grp", "chan"), None, None, "band")
    return jax.shard_map(
        functools.partial(on_device, mesh.shape["chan"]),
        mesh=mesh,
        in_specs=in_specs,
        out_specs=out_specs,
        check_vma=False,
    )
```

time: 344 us -> 110 us (0.32)
  the two profiles are of different devices: /device:TPU:0 before, /device:TPU:31 now
where the time goes in v1:
time: 110 us
  waiting for transfers between devices  57.2 us (52%)
  starting transfers between devices  34.4 us (31%)
  Pallas kernels  14.5 us (13%)
  local copies, waits for them, and re-layouts  3.18 us (3%)
    ppermute x3, waiting for transfers between devices, on_device(): blocks[MEMBERS - distance] = lax.ppermute(chunk, 'chan', route)  36.2 us
    ppermute x7, starting transfers between devices, on_device(): piece = lax.ppermute(piece, ('chan', 'band'), route)  29.6 us
    ppermute x7, waiting for transfers between devices, on_device(): piece = lax.ppermute(piece, ('chan', 'band'), route)  21 us
    pallas_call x1, Pallas kernels, partner_pairs(): pl.pallas_call(pair_kernel, out_shape=(shape,) * (2 * MEMBERS), in_specs=...  5.37 us
    pallas_call x4, Pallas kernels, ordered_chunk(): pl.pallas_call(functools.partial(order_kernel, distance), out_shape=jax.S...  3.44 us
    ppermute x3, starting transfers between devices, on_device(): blocks[MEMBERS - distance] = lax.ppermute(chunk, 'chan', route)  3.44 us
    pallas_call x1, Pallas kernels, self_pairs(): pl.pallas_call(self_kernel, out_shape=(shape, shape), in_specs=[SMEM] + [...  3.11 us
    pallas_call x1, Pallas kernels, lag_transform(): pl.pallas_call(lag_kernel, out_shape=jax.ShapeDtypeStruct((3, lags, colum...  2.56 us
  transfers between devices with their start and end apart: 11, of which 4 were waited for; matrix products, arithmetic and copies ran while one was open for 1% of the time, Pallas kernels for 10%

profile of v1, /device:TPU:31, one launch (start us, length us, event | category | flops | bytes accessed | tf_op | source)
XLA Modules:
  0.0 109.5 jit_solution(11683529038230019156)
XLA Ops:
  0.0 0.0 copy-start
  0.0 0.1 pad_add_fusion.place
  0.1 0.0 copy-start.1
  0.1 1.7 %copy-done.1 = f32[2,16,80,256]{3,2,1,0:T(8,128)S(1)} copy-done((f32[2,16,80,256]{3,2,1,0:T(8,128)S(1)}, f32[2,16,80,256]{3,2,1,0:T(8,128)}, u32[]{:S(2)}) %copy-start.1) | copy-done | bytes 2621464
  1.8 0.0 copy-start.2
  1.8 0.7 copy-done.2
  2.5 0.9 order_3.1.refs_3_
  3.3 0.2 collective-permute-start.1
  3.6 0.9 order_2.1.refs_2_
  4.4 0.1 collective-permute-start.2
  4.5 0.9 order_1.1.refs_1_
  5.4 3.1 %collective-permute-start.3 = (f32[2,4,80,256]{3,2,1,0:T(8,128)S(1)}, f32[2,4,80,256]{3,2,1,0:T(8,128)S(1)}, u32[]{:S(2)}, u32[]{:S(2)}) collective-permute-start(f32[2,4,80,256]{3,2,1,0:T(8,128)S(1)} %order_1.1.refs_1_), channel_id=1, source_target_pairs={{0,4},{2,6},{4,8},{6,10},{8,12},{10,14},{12,0},{14,2},{1,5},{3,7},... | collective-permute-start | bytes 1966088 | tf_op jit(solution)/shard_map/ppermute | solution.py:237
  8.5 0.9 order_0.1.refs_0_
  9.4 3.1 %self_pairs.1 = (f32[32,3200]{1,0:T(8,128)S(1)}, f32[32,3200]{1,0:T(8,128)S(1)}) custom-call(s32[2]{0:T(128)S(1)} %pad_add_fusion.place, f32[2,4,80,256]{3,2,1,0:T(8,128)S(1)} %order_0.1.refs_0_, f32[2,4,80,256]{3,2,1,0:T(8,128)S(1)} %order_1.1.refs_1_, f32[2,4,80,256]{3,2,1,0:T(8,128)S(1)} %order_2.1.refs_2_, f32[2,4,80,256]{3,2,1,0:T(8,128)S(1)} %order_3.1.refs_3_), custom_call_target="tpu_custom_call" | custom-call | flops 5033164800 | bytes 4194304 | tf_op jit(solution)/shard_map/self_pairs/pallas_call | solution.py:149
  12.5 1.3 %collective-permute-start = (f32[32,3200]{1,0:T(8,128)S(1)}, f32[32,3200]{1,0:T(8,128)S(1)}, u32[]{:S(2)}, u32[]{:S(2)}) collective-permute-start(f32[32,3200]{1,0:T(8,128)S(1)} %get-tuple-element.16), channel_id=1, source_target_pairs={{0,1},{1,0},{2,3},{3,2},{4,5},{5,4},{6,7},{7,6},{8,9},{9,8},{10,11... | collective-permute-start | bytes 1228808 | tf_op jit(solution)/shard_map/ppermute | solution.py:241
  13.8 7.1 %collective-permute-done.1.refs_1_ = f32[2,4,80,256]{3,2,1,0:T(8,128)S(1)} collective-permute-done((f32[2,4,80,256]{3,2,1,0:T(8,128)S(1)}, f32[2,4,80,256]{3,2,1,0:T(8,128)S(1)}, u32[]{:S(2)}, u32[]{:S(2)}) %collective-permute-start.1) | collective-permute-done | bytes 655392 | tf_op jit(solution)/shard_map/ppermute | solution.py:237
  20.9 29.1 %collective-permute-done.2.refs_2_ = f32[2,4,80,256]{3,2,1,0:T(8,128)S(1)} collective-permute-done((f32[2,4,80,256]{3,2,1,0:T(8,128)S(1)}, f32[2,4,80,256]{3,2,1,0:T(8,128)S(1)}, u32[]{:S(2)}, u32[]{:S(2)}) %collective-permute-start.2) | collective-permute-done | bytes 655392 | tf_op jit(solution)/shard_map/ppermute | solution.py:237
  50.0 0.0 collective-permute-done.3.refs_3_
  50.0 5.4 %partner_pairs.1 = (f32[2,8,3200]{2,1,0:T(8,128)S(1)}, f32[2,8,3200]{2,1,0:T(8,128)S(1)}, f32[2,8,3200]{2,1,0:T(8,128)S(1)}, f32[2,8,3200]{2,1,0:T(8,128)S(1)}, ...) custom-call(s32[2]{0:T(128)S(1)} %pad_add_fusion.place, ...), custom_call_target="tpu_custom_call" | custom-call | flops 1258291200 | bytes 4194304 | tf_op jit(solution)/shard_map/partner_pairs/pallas_call | solution.py:166
  55.3 12.2 %collective-permute-start.4 = (f32[2,8,3200]{2,1,0:T(8,128)S(1)}, f32[2,8,3200]{2,1,0:T(8,128)S(1)}, u32[]{:S(2)}, u32[]{:S(2)}) collective-permute-start(f32[2,8,3200]{2,1,0:T(8,128)S(1)} %get-tuple-element.18), channel_id=1, source_target_pairs={{0,4},{1,5},{2,6},{3,7},{4,8},{5,9},{6,10},{7,11},{8,12},{9,13},{1... | collective-permute-start | bytes 614408 | tf_op jit(solution)/shard_map/ppermute | solution.py:253
  67.5 3.4 %collective-permute-start.5 = (f32[2,8,3200]{2,1,0:T(8,128)S(1)}, f32[2,8,3200]{2,1,0:T(8,128)S(1)}, u32[]{:S(2)}, u32[]{:S(2)}) collective-permute-start(f32[2,8,3200]{2,1,0:T(8,128)S(1)} %get-tuple-element.19), channel_id=1, source_target_pairs={{0,8},{1,9},{2,10},{3,11},{4,12},{5,13},{6,14},{7,15},{8,0},{9,1},... | collective-permute-start | bytes 614408 | tf_op jit(solution)/shard_map/ppermute | solution.py:253
  70.9 0.0 copy-done
  70.9 0.8 gather_fusion
  71.7 0.1 collective-permute-start.6
  71.8 1.1 %collective-permute-start.7 = (f32[2,8,3200]{2,1,0:T(8,128)S(1)}, f32[2,8,3200]{2,1,0:T(8,128)S(1)}, u32[]{:S(2)}, u32[]{:S(2)}) collective-permute-start(f32[2,8,3200]{2,1,0:T(8,128)S(1)} %get-tuple-element.21), channel_id=1, source_target_pairs={{0,1},{1,0},{2,3},{3,2},{4,5},{5,4},{6,7},{7,6},{8,9},{9,8},{10,11... | collective-permute-start | bytes 614408 | tf_op jit(solution)/shard_map/ppermute | solution.py:253
  72.9 0.0 collective-permute-done.other
  72.9 3.4 %collective-permute-start.8 = (f32[2,8,3200]{2,1,0:T(8,128)S(1)}, f32[2,8,3200]{2,1,0:T(8,128)S(1)}, u32[]{:S(2)}, u32[]{:S(2)}) collective-permute-start(f32[2,8,3200]{2,1,0:T(8,128)S(1)} %get-tuple-element.22), channel_id=1, source_target_pairs={{0,5},{1,4},{2,7},{3,6},{4,9},{5,8},{6,11},{7,10},{8,13},{9,12},{1... | collective-permute-start | bytes 614408 | tf_op jit(solution)/shard_map/ppermute | solution.py:253
  76.2 0.0 collective-permute-done.4.refs_1_
  76.2 9.6 %collective-permute-start.9 = (f32[2,8,3200]{2,1,0:T(8,128)S(1)}, f32[2,8,3200]{2,1,0:T(8,128)S(1)}, u32[]{:S(2)}, u32[]{:S(2)}) collective-permute-start(f32[2,8,3200]{2,1,0:T(8,128)S(1)} %get-tuple-element.23), channel_id=1, source_target_pairs={{0,9},{1,8},{2,11},{3,10},{4,13},{5,12},{6,15},{7,14},{8,1},{9,0},... | collective-permute-start | bytes 614408 | tf_op jit(solution)/shard_map/ppermute | solution.py:253
  85.8 3.0 %collective-permute-done.5.refs_2_ = f32[2,8,3200]{2,1,0:T(8,128)S(1)} collective-permute-done((f32[2,8,3200]{2,1,0:T(8,128)S(1)}, f32[2,8,3200]{2,1,0:T(8,128)S(1)}, u32[]{:S(2)}, u32[]{:S(2)}) %collective-permute-start.5) | collective-permute-done | bytes 204832 | tf_op jit(solution)/shard_map/ppermute | solution.py:253
  88.8 0.0 collective-permute-start.10
  88.8 0.2 select_multiply_fusion.table
  88.9 0.0 collective-permute-done.6.refs_3_
  89.0 0.0 collective-permute-done.7.refs_4_
  89.0 0.0 collective-permute-done.8.refs_5_
  89.0 18.0 %collective-permute-done.9.refs_6_ = f32[2,8,3200]{2,1,0:T(8,128)S(1)} collective-permute-done((f32[2,8,3200]{2,1,0:T(8,128)S(1)}, f32[2,8,3200]{2,1,0:T(8,128)S(1)}, u32[]{:S(2)}, u32[]{:S(2)}) %collective-permute-start.9) | collective-permute-done | bytes 204832 | tf_op jit(solution)/shard_map/ppermute | solution.py:253
  107.0 0.0 collective-permute-done.10.refs_7_
  107.0 2.6 %lag_transform.1 = f32[3,64,3200]{2,1,0:T(8,128)} custom-call(f32[64,64]{1,0:T(8,128)S(1)} %select_multiply_fusion.table, f32[32,3200]{1,0:T(8,128)S(1)} %get-tuple-element.15.same, f32[32,3200]{1,0:T(8,128)S(1)} %collective-permute-done.other, f32[2,8,3200]{2,1,0:T(8,128)S(1)} %get-tuple-element.17.refs_0_, ...), custom_call_target="tpu_custom_call" | custom-call | tf_op jit(solution)/shard_map/lag_transform/pallas_call | solution.py:198
  (3 shorter events, 0.0 us)
Async XLA Ops:
  0.0 70.9 %copy-start = (s32[32]{0:T(128)S(1)}, s32[32]{0:T(128)}, u32[]{:S(2)}) copy-start(s32[32]{0:T(128)} %param.5) | copy-start | bytes 388
  0.1 1.7 %copy-start.1 = (f32[2,16,80,256]{3,2,1,0:T(8,128)S(1)}, f32[2,16,80,256]{3,2,1,0:T(8,128)}, u32[]{:S(2)}) copy-start(f32[2,16,80,256]{3,2,1,0:T(8,128)} %spectra.7) | copy-start | bytes 7864324
  1.8 0.7 copy-start.2
  3.3 17.5 %collective-permute-start.1 = (f32[2,4,80,256]{3,2,1,0:T(8,128)S(1)}, f32[2,4,80,256]{3,2,1,0:T(8,128)S(1)}, u32[]{:S(2)}, u32[]{:S(2)}) collective-permute-start(f32[2,4,80,256]{3,2,1,0:T(8,128)S(1)} %order_3.1.refs_3_), channel_id=1, source_target_pairs={{0,12},{2,14},{4,0},{6,2},{8,4},{10,6},{12,8},{14,10},{1,13},{3,15... | collective-permute-start | bytes 1966088 | tf_op jit(solution)/shard_map/ppermute | solution.py:237
  4.4 45.6 %collective-permute-start.2 = (f32[2,4,80,256]{3,2,1,0:T(8,128)S(1)}, f32[2,4,80,256]{3,2,1,0:T(8,128)S(1)}, u32[]{:S(2)}, u32[]{:S(2)}) collective-permute-start(f32[2,4,80,256]{3,2,1,0:T(8,128)S(1)} %order_2.1.refs_2_), channel_id=1, source_target_pairs={{0,8},{2,10},{4,12},{6,14},{8,0},{10,2},{12,4},{14,6},{1,9},{3,11}... | collective-permute-start | bytes 1966088 | tf_op jit(solution)/shard_map/ppermute | solution.py:237
  5.4 44.6 %collective-permute-start.3 = (f32[2,4,80,256]{3,2,1,0:T(8,128)S(1)}, f32[2,4,80,256]{3,2,1,0:T(8,128)S(1)}, u32[]{:S(2)}, u32[]{:S(2)}) collective-permute-start(f32[2,4,80,256]{3,2,1,0:T(8,128)S(1)} %order_1.1.refs_1_), channel_id=1, source_target_pairs={{0,4},{2,6},{4,8},{6,10},{8,12},{10,14},{12,0},{14,2},{1,5},{3,7},... | collective-permute-start | bytes 1966088 | tf_op jit(solution)/shard_map/ppermute | solution.py:237
  12.5 60.4 %collective-permute-start = (f32[32,3200]{1,0:T(8,128)S(1)}, f32[32,3200]{1,0:T(8,128)S(1)}, u32[]{:S(2)}, u32[]{:S(2)}) collective-permute-start(f32[32,3200]{1,0:T(8,128)S(1)} %get-tuple-element.16), channel_id=1, source_target_pairs={{0,1},{1,0},{2,3},{3,2},{4,5},{5,4},{6,7},{7,6},{8,9},{9,8},{10,11... | collective-permute-start | bytes 1228808 | tf_op jit(solution)/shard_map/ppermute | solution.py:241
  55.3 20.9 %collective-permute-start.4 = (f32[2,8,3200]{2,1,0:T(8,128)S(1)}, f32[2,8,3200]{2,1,0:T(8,128)S(1)}, u32[]{:S(2)}, u32[]{:S(2)}) collective-permute-start(f32[2,8,3200]{2,1,0:T(8,128)S(1)} %get-tuple-element.18), channel_id=1, source_target_pairs={{0,4},{1,5},{2,6},{3,7},{4,8},{5,9},{6,10},{7,11},{8,12},{9,13},{1... | collective-permute-start | bytes 614408 | tf_op jit(solution)/shard_map/ppermute | solution.py:253
  67.5 21.3 %collective-permute-start.5 = (f32[2,8,3200]{2,1,0:T(8,128)S(1)}, f32[2,8,3200]{2,1,0:T(8,128)S(1)}, u32[]{:S(2)}, u32[]{:S(2)}) collective-permute-start(f32[2,8,3200]{2,1,0:T(8,128)S(1)} %get-tuple-element.19), channel_id=1, source_target_pairs={{0,8},{1,9},{2,10},{3,11},{4,12},{5,13},{6,14},{7,15},{8,0},{9,1},... | collective-permute-start | bytes 614408 | tf_op jit(solution)/shard_map/ppermute | solution.py:253
  71.7 17.2 %collective-permute-start.6 = (f32[2,8,3200]{2,1,0:T(8,128)S(1)}, f32[2,8,3200]{2,1,0:T(8,128)S(1)}, u32[]{:S(2)}, u32[]{:S(2)}) collective-permute-start(f32[2,8,3200]{2,1,0:T(8,128)S(1)} %get-tuple-element.20), channel_id=1, source_target_pairs={{0,12},{1,13},{2,14},{3,15},{4,0},{5,1},{6,2},{7,3},{8,4},{9,5},{1... | collective-permute-start | bytes 614408 | tf_op jit(solution)/shard_map/ppermute | solution.py:253
  71.8 17.2 %collective-permute-start.7 = (f32[2,8,3200]{2,1,0:T(8,128)S(1)}, f32[2,8,3200]{2,1,0:T(8,128)S(1)}, u32[]{:S(2)}, u32[]{:S(2)}) collective-permute-start(f32[2,8,3200]{2,1,0:T(8,128)S(1)} %get-tuple-element.21), channel_id=1, source_target_pairs={{0,1},{1,0},{2,3},{3,2},{4,5},{5,4},{6,7},{7,6},{8,9},{9,8},{10,11... | collective-permute-start | bytes 614408 | tf_op jit(solution)/shard_map/ppermute | solution.py:253
  72.9 16.1 %collective-permute-start.8 = (f32[2,8,3200]{2,1,0:T(8,128)S(1)}, f32[2,8,3200]{2,1,0:T(8,128)S(1)}, u32[]{:S(2)}, u32[]{:S(2)}) collective-permute-start(f32[2,8,3200]{2,1,0:T(8,128)S(1)} %get-tuple-element.22), channel_id=1, source_target_pairs={{0,5},{1,4},{2,7},{3,6},{4,9},{5,8},{6,11},{7,10},{8,13},{9,12},{1... | collective-permute-start | bytes 614408 | tf_op jit(solution)/shard_map/ppermute | solution.py:253
  76.2 30.7 %collective-permute-start.9 = (f32[2,8,3200]{2,1,0:T(8,128)S(1)}, f32[2,8,3200]{2,1,0:T(8,128)S(1)}, u32[]{:S(2)}, u32[]{:S(2)}) collective-permute-start(f32[2,8,3200]{2,1,0:T(8,128)S(1)} %get-tuple-element.23), channel_id=1, source_target_pairs={{0,9},{1,8},{2,11},{3,10},{4,13},{5,12},{6,15},{7,14},{8,1},{9,0},... | collective-permute-start | bytes 614408 | tf_op jit(solution)/shard_map/ppermute | solution.py:253
  88.8 18.2 %collective-permute-start.10 = (f32[2,8,3200]{2,1,0:T(8,128)S(1)}, f32[2,8,3200]{2,1,0:T(8,128)S(1)}, u32[]{:S(2)}, u32[]{:S(2)}) collective-permute-start(f32[2,8,3200]{2,1,0:T(8,128)S(1)} %get-tuple-element.24), channel_id=1, source_target_pairs={{0,13},{1,12},{2,15},{3,14},{4,1},{5,0},{6,3},{7,2},{8,5},{9,4},{1... | collective-permute-start | bytes 614408 | tf_op jit(solution)/shard_map/ppermute | solution.py:253

commit v2 on v1

--- a/solution.py
+++ b/solution.py
@@ -13,6 +13,20 @@
 BF16 = jnp.bfloat16
 VMEM = pl.BlockSpec(memory_space=pltpu.VMEM)
 SMEM = pl.BlockSpec(memory_space=pltpu.SMEM)
+PIECES = [
+    (2, 0, (1,)),
+    (2, 1, (1,)),
+    (2, 0, (0,)),
+    (2, 1, (0,)),
+    (1, 0, (1,)),
+    (1, 1, (1,)),
+    (3, 0, (0, 1)),
+    (3, 1, (0, 1)),
+    (1, 0, (0,)),
+    (1, 1, (0,)),
+    (0, 1, (0, 1)),
+    (0, 0, (0, 1)),
+]
 LIMIT = 40 * 1024 * 1024
 
 
@@ -34,9 +48,9 @@
     return lax.dot_general(left, right, (dims, ((), ())), preferred_element_type=F32)
 
 
-def order_kernel(distance, place, order, spectra, ordered):
+def order_kernel(which, place, order, spectra, ordered):
     parts, bins, rows, _ = ordered.shape
-    chunk = lax.rem(place[0] + distance, MEMBERS)
+    chunk = place[2 + which]
     row_ids = lax.broadcasted_iota(jnp.int32, (rows, rows), 0)
     chosen = jnp.where(row_ids == order[...], 1.0, 0.0).astype(BF16)
     chosen = jnp.concatenate([chosen] * 3, axis=0)
@@ -47,15 +61,15 @@
             ordered[part, slot] = dot(chosen, stacked, ((0,), (0,)))
 
 
-def ordered_chunk(place, order, spectra, distance):
+def ordered_chunk(place, order, spectra, which):
     parts, bins, rows, windows = spectra.shape
     return pl.pallas_call(
-        functools.partial(order_kernel, distance),
+        functools.partial(order_kernel, which),
         out_shape=jax.ShapeDtypeStruct((parts, bins // MEMBERS, rows, windows), F32),
         in_specs=[SMEM, VMEM, VMEM],
         out_specs=VMEM,
         compiler_params=pltpu.CompilerParams(vmem_limit_bytes=LIMIT),
-        name=f"order_{distance}",
+        name=f"order_{which}",
     )(place, order, spectra)
 
 
@@ -131,14 +145,32 @@
                 scratch[owner * 2 + pair, slot * 2 * rows : (slot + 1) * 2 * rows, 0:rows] = (
                     product(lefts[owner], rights[partner])
                 )
-    for owner in range(MEMBERS):
-        for shift in range(2):
-            first = lax.rem(place[1] + shift, 2) * half
-            for pair in range(2):
-                for group in range(half // 8):
-                    outs[owner * 2 + shift][pair, :, group * width : (group + 1) * width] = (
-                        packed_rows(scratch, owner * 2 + pair, first, rows, group, count)
-                    )
+    for at, (owner, shift, pairs) in enumerate(PIECES):
+        first = lax.rem(place[1] + shift, 2) * half
+        for row, pair in enumerate(pairs):
+            for group in range(half // 8):
+                outs[at][row, :, group * width : (group + 1) * width] = (
+                    packed_rows(scratch, owner * 2 + pair, first, rows, group, count)
+                )
+
+
+def extra_kernel(place, mine, theirs, same, other, scratch):
+    _, bins, rows, _ = mine.shape
+    half = rows // 2
+    count = 2 * bins
+    width = 8 * rows
+    even = lax.rem(place[0], 2) == 0
+    for slot in range(bins):
+        first = [jnp.where(even, mine[part, slot], theirs[part, slot]) for part in range(2)]
+        second = [jnp.where(even, theirs[part, slot], mine[part, slot]) for part in range(2)]
+        value = product(left_operand(*first), right_operand(*second))
+        scratch[0, slot * 2 * rows : (slot + 1) * 2 * rows, 0:rows] = value
+    for out, shift in ((same, 0), (other, 1)):
+        start = lax.rem(place[1] + shift, 2) * half
+        for group in range(half // 8):
+            out[0, :, group * width : (group + 1) * width] = (
+                packed_rows(scratch, 0, start, rows, group, count)
+            )
 
 
 def self_pairs(place, chunks):
@@ -161,13 +193,15 @@
 def partner_pairs(place, blocks):
     _, bins, rows, windows = blocks[0].shape
     columns = rows * rows // 2
-    shape = jax.ShapeDtypeStruct((2, 2 * bins, columns), F32)
+    shapes = tuple(
+        jax.ShapeDtypeStruct((len(pairs), 2 * bins, columns), F32) for _, _, pairs in PIECES
+    )
     flops = 2 * MEMBERS * bins * 3 * 2 * 4 * rows * rows * windows
     return pl.pallas_call(
         pair_kernel,
-        out_shape=(shape,) * (2 * MEMBERS),
+        out_shape=shapes,
         in_specs=[SMEM] + [VMEM] * MEMBERS,
-        out_specs=(VMEM,) * (2 * MEMBERS),
+        out_specs=(VMEM,) * len(PIECES),
         scratch_shapes=[pltpu.VMEM((2 * MEMBERS, 2 * bins * rows, 128), F32)],
         compiler_params=pltpu.CompilerParams(vmem_limit_bytes=LIMIT),
         cost_estimate=pl.CostEstimate(flops=flops, bytes_accessed=1 << 22, transcendentals=0),
@@ -175,34 +209,63 @@
     )(place, *blocks)
 
 
-def lag_kernel(table, same, other, *refs):
-    pieces, out = refs[:-1], refs[-1]
+def extra_pairs(place, mine, theirs):
+    _, bins, rows, windows = mine.shape
+    shape = jax.ShapeDtypeStruct((1, 2 * bins, rows * rows // 2), F32)
+    return pl.pallas_call(
+        extra_kernel,
+        out_shape=(shape, shape),
+        in_specs=[SMEM, VMEM, VMEM],
+        out_specs=(VMEM, VMEM),
+        scratch_shapes=[pltpu.VMEM((1, 2 * bins * rows, 128), F32)],
+        compiler_params=pltpu.CompilerParams(vmem_limit_bytes=LIMIT),
+        name="extra_pairs",
+    )(place, mine, theirs)
+
+
+def lag_kernel(place, table, same, other, *refs):
+    pieces, extras, out = refs[: len(PIECES)], refs[len(PIECES) : -1], refs[-1]
     columns = out.shape[2]
     tile = 640 if columns % 640 == 0 else columns
     high, low = halves(table[...])
     dims = ((1,), (0,))
+    even = lax.rem(place[0], 2) == 0
+    found = {}
+    for piece, (distance, shift, pairs) in zip(pieces, PIECES):
+        for row, pair in enumerate(pairs):
+            found[pair, shift, distance] = piece, row
+    own_same, own_other, theirs_same, theirs_other = extras
+    more = {(1, 0): theirs_same, (1, 1): theirs_other, (2, 0): own_same, (2, 1): own_other}
     for pair in range(3):
         for at in range(0, columns, tile):
             span = slice(at, at + tile)
             if pair == 0:
                 stacked = jnp.concatenate([same[:, span], other[:, span]], axis=0)
             else:
-                stacked = jnp.concatenate([piece[pair - 1, :, span] for piece in pieces], axis=0)
+                terms = []
+                for shift in range(2):
+                    for distance in range(MEMBERS):
+                        piece, row = found[pair - 1, shift, distance]
+                        term = piece[row, :, span]
+                        if pair == 1 and (distance, shift) in more:
+                            term = jnp.where(even, more[distance, shift][0, :, span], term)
+                        terms.append(term)
+                stacked = jnp.concatenate(terms, axis=0)
             first, second = halves(stacked)
             out[pair, :, span] = dot(high, first, dims) + dot(high, second, dims) + dot(low, first, dims)
 
 
-def lag_transform(table, same, other, pieces):
+def lag_transform(place, table, same, other, pieces):
     lags = table.shape[0]
     columns = same.shape[1]
     return pl.pallas_call(
         lag_kernel,
         out_shape=jax.ShapeDtypeStruct((3, lags, columns), F32),
-        in_specs=[VMEM] * (3 + len(pieces)),
+        in_specs=[SMEM] + [VMEM] * (3 + len(pieces)),
         out_specs=VMEM,
         compiler_params=pltpu.CompilerParams(vmem_limit_bytes=LIMIT),
         name="lag_transform",
-    )(table, same, other, *pieces)
+    )(place, table, same, other, *pieces)
 
 
 def lag_table(bin_assign, member, band, factor):
@@ -221,39 +284,54 @@
     return jnp.where(part[None, :] == 0, jnp.cos(angles), -jnp.sin(angles)) * factor
 
 
+def moved(array, loop_size, distance, shift, wanted):
+    quarter = loop_size // MEMBERS
+    route = [
+        (i * 2 + j, (i + distance(i // quarter) * quarter) % loop_size * 2 + (j + shift) % 2)
+        for i in range(loop_size)
+        for j in range(2)
+        if wanted(i // quarter)
+    ]
+    return lax.ppermute(array, ("chan", "band"), route)
+
+
 def on_device(loop_size, spectra, channel_order, bin_assign):
-    quarter = loop_size // MEMBERS
-    chan = lax.axis_index("chan")
+    member = lax.axis_index("chan") // (loop_size // MEMBERS)
     band = lax.axis_index("band")
-    member = chan // quarter
-    place = jnp.stack([member, band]).astype(jnp.int32)
+    even = member % 2 == 0
+    every = lambda m: True
+    away = [lax.rem(member + distance, MEMBERS) for distance in range(MEMBERS)]
+    swapped = jnp.where(even, away[3], away[1])
+    place = jnp.stack([member, band, *away, swapped]).astype(jnp.int32)
     blocks = [None] * MEMBERS
     chunks = [None] * MEMBERS
-    for distance in (2, 3, 1, 0):
-        chunk = ordered_chunk(place, channel_order, spectra, distance)
-        chunks[distance] = chunk
-        if distance:
-            route = [(i, (i + distance * quarter) % loop_size) for i in range(loop_size)]
-            blocks[MEMBERS - distance] = lax.ppermute(chunk, "chan", route)
-        else:
-            blocks[0] = chunk
+    for distance in (2, 3, 1):
+        chunks[distance] = ordered_chunk(place, channel_order, spectra, distance)
+        blocks[MEMBERS - distance] = moved(
+            chunks[distance], loop_size, lambda m: distance, 0, every
+        )
+    swap = ordered_chunk(place, channel_order, spectra, MEMBERS)
+    theirs = moved(swap, loop_size, lambda m: 1 if m % 2 == 0 else -1, 0, every)
+    blocks[0] = chunks[0] = ordered_chunk(place, channel_order, spectra, 0)
     same, other = self_pairs(place, chunks)
-    other = lax.ppermute(other, "band", [(0, 1), (1, 0)])
+    other = moved(other, loop_size, lambda m: 0, 1, every)
+    own_same, own_other = extra_pairs(place, chunks[2], theirs)
+    odd = lambda m: m % 2 == 1
+    theirs_same = moved(own_same, loop_size, lambda m: -1, 0, odd)
+    theirs_other = moved(own_other, loop_size, lambda m: -1, 1, odd)
+    own_other = moved(own_other, loop_size, lambda m: 0, 1, every)
     results = partner_pairs(place, blocks)
     pieces = []
-    for shift in range(2):
-        for distance in range(MEMBERS):
-            piece = results[distance * 2 + shift]
-            if distance or shift:
-                route = [
-                    (i * 2 + j, (i + distance * quarter) % loop_size * 2 + (j + shift) % 2)
-                    for i in range(loop_size)
-                    for j in range(2)
-                ]
-                piece = lax.ppermute(piece, ("chan", "band"), route)
-            pieces.append(piece)
+    for piece, (distance, shift, pairs) in zip(results, PIECES):
+        wanted = every
+        if pairs == (0,):
+            wanted = lambda m: (m + distance) % 2 == 1
+        if distance or shift:
+            piece = moved(piece, loop_size, lambda m: distance, shift, wanted)
+        pieces.append(piece)
+    pieces += [own_same, own_other, theirs_same, theirs_other]
     table = lag_table(bin_assign, member, band, 1.0 / spectra.shape[3])
-    return lag_transform(table, same, other, pieces)[None]
+    return lag_transform(place, table, same, other, pieces)[None]
 
 
 def solution(mesh):

time: 110 us -> 118 us (1.073)
  the two profiles are of different devices: /device:TPU:31 before, /device:TPU:0 now
where the time goes in v2:
time: 118 us
  waiting for transfers between devices  63.6 us (54%)
  starting transfers between devices  29.1 us (25%)
  Pallas kernels  18.1 us (15%)
  local copies, waits for them, and re-layouts  6.53 us (6%)
    ppermute x19, waiting for transfers between devices, moved(): return lax.ppermute(array, ('chan', 'band'), route)  63.6 us
    ppermute x19, starting transfers between devices, moved(): return lax.ppermute(array, ('chan', 'band'), route)  29.1 us
    pallas_call x1, Pallas kernels, partner_pairs(): pl.pallas_call(pair_kernel, out_shape=shapes, in_specs=[SMEM] + [VMEM] *...  6.09 us
    unnamed x16, local copies, waits for them, and re-layouts  5.68 us
    pallas_call x5, Pallas kernels, ordered_chunk(): pl.pallas_call(functools.partial(order_kernel, which), out_shape=jax.Shap...  4.31 us
    pallas_call x1, Pallas kernels, self_pairs(): pl.pallas_call(self_kernel, out_shape=(shape, shape), in_specs=[SMEM] + [...  3.12 us
    pallas_call x1, Pallas kernels, lag_transform(): pl.pallas_call(lag_kernel, out_shape=jax.ShapeDtypeStruct((3, lags, colum...  3.12 us
  transfers between devices with their start and end apart: 19, of which 6 were waited for; matrix products, arithmetic and copies ran while one was open for 1% of the time, Pallas kernels for 12%

profile of v2, /device:TPU:0, one launch (start us, length us, event | category | flops | bytes accessed | tf_op | source)
XLA Modules:
  0.0 117.6 jit_solution(16225170544056579363)
XLA Ops:
  0.0 0.0 copy-start
  0.0 0.1 stack.31.place
  0.1 0.0 copy-start.1
  0.1 1.7 %copy-done.1 = f32[2,16,80,256]{3,2,1,0:T(8,128)S(1)} copy-done((f32[2,16,80,256]{3,2,1,0:T(8,128)S(1)}, f32[2,16,80,256]{3,2,1,0:T(8,128)}, u32[]{:S(2)}) %copy-start.1) | copy-done | bytes 2621464
  1.8 0.0 copy-start.2
  1.8 0.7 copy-done.2
  2.5 0.9 order_3.1.refs_3_
  3.3 5.1 %collective-permute-start.1 = (f32[2,4,80,256]{3,2,1,0:T(8,128)S(1)}, f32[2,4,80,256]{3,2,1,0:T(8,128)S(1)}, u32[]{:S(2)}, u32[]{:S(2)}) collective-permute-start(f32[2,4,80,256]{3,2,1,0:T(8,128)S(1)} %order_3.1.refs_3_), channel_id=1, source_target_pairs={{0,12},{1,13},{2,14},{3,15},{4,0},{5,1},{6,2},{7,3},{8,4},{9,5},{1... | collective-permute-start | bytes 1966088 | tf_op jit(solution)/shard_map/ppermute | solution.py:295
  8.4 0.9 order_2.1.refs_2_.mine
  9.3 0.1 collective-permute-start.2
  9.4 0.9 order_1.1.refs_1_
  10.3 1.1 collective-permute-start.3
  11.3 0.9 order_4.1
  12.2 2.5 %collective-permute-start.15 = (f32[2,4,80,256]{3,2,1,0:T(8,128)S(1)}, f32[2,4,80,256]{3,2,1,0:T(8,128)S(1)}, u32[]{:S(2)}, u32[]{:S(2)}) collective-permute-start(f32[2,4,80,256]{3,2,1,0:T(8,128)S(1)} %order_4.1), channel_id=1, source_target_pairs={{0,4},{1,5},{2,6},{3,7},{4,0},{5,1},{6,2},{7,3},{8,12},{9,13},{10,... | collective-permute-start | bytes 1966088 | tf_op jit(solution)/shard_map/ppermute | solution.py:295
  14.7 0.9 order_0.1.refs_0_
  15.6 3.1 %self_pairs.1 = (f32[32,3200]{1,0:T(8,128)S(1)}, f32[32,3200]{1,0:T(8,128)S(1)}) custom-call(s32[7]{0:T(128)S(1)} %stack.31.place, f32[2,4,80,256]{3,2,1,0:T(8,128)S(1)} %order_0.1.refs_0_, f32[2,4,80,256]{3,2,1,0:T(8,128)S(1)} %order_1.1.refs_1_, f32[2,4,80,256]{3,2,1,0:T(8,128)S(1)} %order_2.1.refs_2_.mine, f32[2,4,80,256]{3,2,1,0:T(8,128)S(1)} %order_3.1.refs_3_), custom_call_target="tpu_custom_call" | custom-call | flops 5033164800 | bytes 4194304 | tf_op jit(solution)/shard_map/self_pairs/pallas_call | solution.py:181
  18.7 0.1 collective-permute-start
  18.8 4.9 %collective-permute-done.1.refs_1_ = f32[2,4,80,256]{3,2,1,0:T(8,128)S(1)} collective-permute-done((f32[2,4,80,256]{3,2,1,0:T(8,128)S(1)}, f32[2,4,80,256]{3,2,1,0:T(8,128)S(1)}, u32[]{:S(2)}, u32[]{:S(2)}) %collective-permute-start.1) | collective-permute-done | bytes 655392 | tf_op jit(solution)/shard_map/ppermute | solution.py:295
  23.7 40.8 %collective-permute-done.2.refs_2_ = f32[2,4,80,256]{3,2,1,0:T(8,128)S(1)} collective-permute-done((f32[2,4,80,256]{3,2,1,0:T(8,128)S(1)}, f32[2,4,80,256]{3,2,1,0:T(8,128)S(1)}, u32[]{:S(2)}, u32[]{:S(2)}) %collective-permute-start.2) | collective-permute-done | bytes 655392 | tf_op jit(solution)/shard_map/ppermute | solution.py:295
  64.5 0.0 collective-permute-done.3.refs_3_
  64.5 6.1 %partner_pairs.1 = (f32[1,8,3200]{2,1,0:T(8,128)}, f32[1,8,3200]{2,1,0:T(8,128)}, f32[1,8,3200]{2,1,0:T(8,128)}, f32[1,8,3200]{2,1,0:T(8,128)}, f32[1,8,3200]{2,...) custom-call(s32[7]{0:T(128)S(1)} %stack.31.place, ...), custom_call_target="tpu_custom_call" | custom-call | flops 1258291200 | bytes 4194304 | tf_op jit(solution)/shard_map/partner_pairs/pallas_call | solution.py:200
  70.6 0.0 copy-start.3
  70.6 0.7 copy-done.3
  71.2 0.0 copy-start.4
  71.2 0.7 copy-done.4
  71.9 0.0 copy-start.5
  71.9 0.6 copy-done.5
  72.6 0.6 copy-done.6
  73.2 0.6 copy-done.7
  73.8 3.6 %collective-permute-start.4 = (f32[1,8,3200]{2,1,0:T(8,128)}, f32[1,8,3200]{2,1,0:T(8,128)S(1)}, u32[]{:S(2)}, u32[]{:S(2)}) collective-permute-start(f32[1,8,3200]{2,1,0:T(8,128)} %get-tuple-element.23), channel_id=1, source_target_pairs={{0,8},{1,9},{2,10},{3,11},{4,12},{5,13},{6,14},{7,15},{8,0},{9,1},... | collective-permute-start | bytes 307208 | tf_op jit(solution)/shard_map/ppermute | solution.py:295
  77.4 0.0 collective-permute-start.5
  77.4 0.7 collective-permute-start.6
  78.1 0.0 collective-permute-done.15.theirs
  78.1 0.7 collective-permute-start.7
  78.8 0.0 copy-done
  78.8 0.8 gather_fusion
  79.6 1.4 %extra_pairs.1 = (f32[1,8,3200]{2,1,0:T(8,128)S(1)}, f32[1,8,3200]{2,1,0:T(8,128)S(1)}) custom-call(s32[7]{0:T(128)S(1)} %stack.31.place, f32[2,4,80,256]{3,2,1,0:T(8,128)S(1)} %order_2.1.refs_2_.mine, f32[2,4,80,256]{3,2,1,0:T(8,128)S(1)} %collective-permute-done.15.theirs), custom_call_target="tpu_custom_call" | custom-call | tf_op jit(solution)/shard_map/extra_pairs/pallas_call | solution.py:215
  81.0 0.0 collective-permute-done.other
  81.0 5.9 %collective-permute-start.8 = (f32[1,8,3200]{2,1,0:T(8,128)}, f32[1,8,3200]{2,1,0:T(8,128)S(1)}, u32[]{:S(2)}, u32[]{:S(2)}) collective-permute-start(f32[1,8,3200]{2,1,0:T(8,128)} %copy-done.7), channel_id=1, source_target_pairs={{0,4},{1,5},{2,6},{3,7},{4,8},{5,9},{6,10},{7,11},{8,12},{9,13},{1... | collective-permute-start | bytes 307208 | tf_op jit(solution)/shard_map/ppermute | solution.py:295
  86.9 5.0 %collective-permute-done.4.refs_0_ = f32[1,8,3200]{2,1,0:T(8,128)S(1)} collective-permute-done((f32[1,8,3200]{2,1,0:T(8,128)}, f32[1,8,3200]{2,1,0:T(8,128)S(1)}, u32[]{:S(2)}, u32[]{:S(2)}) %collective-permute-start.4) | collective-permute-done | bytes 102432 | tf_op jit(solution)/shard_map/ppermute | solution.py:295
  91.9 0.0 collective-permute-start.9
  91.9 1.7 %collective-permute-done.5.refs_1_ = f32[1,8,3200]{2,1,0:T(8,128)S(1)} collective-permute-done((f32[1,8,3200]{2,1,0:T(8,128)}, f32[1,8,3200]{2,1,0:T(8,128)S(1)}, u32[]{:S(2)}, u32[]{:S(2)}) %collective-permute-start.5) | collective-permute-done | bytes 102432 | tf_op jit(solution)/shard_map/ppermute | solution.py:295
  93.6 1.3 %collective-permute-start.12 = (f32[1,8,3200]{2,1,0:T(8,128)}, f32[1,8,3200]{2,1,0:T(8,128)S(1)}, u32[]{:S(2)}, u32[]{:S(2)}) collective-permute-start(f32[1,8,3200]{2,1,0:T(8,128)} %copy-done.5), channel_id=1, source_target_pairs={{0,4},{1,5},{2,6},{3,7},{8,12},{9,13},{10,14},{11,15},{16,20},{17,... | collective-permute-start | bytes 307208 | tf_op jit(solution)/shard_map/ppermute | solution.py:295
  94.9 0.0 collective-permute-done.6.refs_2_
  94.9 1.3 %collective-permute-start.13 = (f32[1,8,3200]{2,1,0:T(8,128)S(1)}, f32[1,8,3200]{2,1,0:T(8,128)S(1)}, u32[]{:S(2)}, u32[]{:S(2)}) collective-permute-start(f32[1,8,3200]{2,1,0:T(8,128)S(1)} %get-tuple-element.32), channel_id=1, source_target_pairs={{0,5},{1,4},{2,7},{3,6},{8,13},{9,12},{10,15},{11,14},{16,21},{17,... | collective-permute-start | bytes 307208 | tf_op jit(solution)/shard_map/ppermute | solution.py:295
  96.2 0.0 collective-permute-done.7.refs_3_
  96.2 0.2 collective-permute-start.16
  96.4 0.0 collective-permute-done.8.refs_4_
  96.4 1.3 %collective-permute-start.18 = (f32[1,8,3200]{2,1,0:T(8,128)S(1)}, f32[1,8,3200]{2,1,0:T(8,128)S(1)}, u32[]{:S(2)}, u32[]{:S(2)}) collective-permute-start(f32[1,8,3200]{2,1,0:T(8,128)S(1)} %get-tuple-element.36), channel_id=1, source_target_pairs={{4,1},{5,0},{6,3},{7,2},{12,9},{13,8},{14,11},{15,10},{20,17},{21,... | collective-permute-start | bytes 307208 | tf_op jit(solution)/shard_map/ppermute | solution.py:295
  97.7 1.2 %collective-permute-done.9.refs_5_ = f32[1,8,3200]{2,1,0:T(8,128)S(1)} collective-permute-done((f32[1,8,3200]{2,1,0:T(8,128)}, f32[1,8,3200]{2,1,0:T(8,128)S(1)}, u32[]{:S(2)}, u32[]{:S(2)}) %collective-permute-start.9) | collective-permute-done | bytes 102432 | tf_op jit(solution)/shard_map/ppermute | solution.py:295
  98.9 4.0 %collective-permute-start.10 = (f32[2,8,3200]{2,1,0:T(8,128)}, f32[2,8,3200]{2,1,0:T(8,128)S(1)}, u32[]{:S(2)}, u32[]{:S(2)}) collective-permute-start(f32[2,8,3200]{2,1,0:T(8,128)} %copy-done.4), channel_id=1, source_target_pairs={{0,12},{1,13},{2,14},{3,15},{4,0},{5,1},{6,2},{7,3},{8,4},{9,5},{1... | collective-permute-start | bytes 614408 | tf_op jit(solution)/shard_map/ppermute | solution.py:295
  102.9 0.0 collective-permute-done.12.refs_8_
  102.9 0.0 collective-permute-start.11
  102.9 0.0 collective-permute-done.13.refs_9_
  102.9 0.2 collective-permute-start.14
  103.1 0.0 collective-permute-done.16.refs_13_
  103.1 1.3 %collective-permute-start.17 = (f32[1,8,3200]{2,1,0:T(8,128)S(1)}, f32[1,8,3200]{2,1,0:T(8,128)S(1)}, u32[]{:S(2)}, u32[]{:S(2)}) collective-permute-start(f32[1,8,3200]{2,1,0:T(8,128)S(1)} %get-tuple-element.35.refs_12_), channel_id=1, source_target_pairs={{4,0},{5,1},{6,2},{7,3},{12,8},{13,9},{14,10},{15,11},{20,16},{21,... | collective-permute-start | bytes 307208 | tf_op jit(solution)/shard_map/ppermute | solution.py:295
  104.4 0.2 select_multiply_fusion.table
  104.5 10.0 %collective-permute-done.17.refs_14_ = f32[1,8,3200]{2,1,0:T(8,128)S(1)} collective-permute-done((f32[1,8,3200]{2,1,0:T(8,128)S(1)}, f32[1,8,3200]{2,1,0:T(8,128)S(1)}, u32[]{:S(2)}, u32[]{:S(2)}) %collective-permute-start.17) | collective-permute-done | bytes 102432 | tf_op jit(solution)/shard_map/ppermute | solution.py:295
  114.5 0.0 collective-permute-done.18.refs_15_
  114.5 0.0 collective-permute-done.10.refs_6_
  114.5 0.0 collective-permute-done.11.refs_7_
  114.5 0.0 collective-permute-done.14.refs_10_
  114.5 3.1 %lag_transform.1 = f32[3,64,3200]{2,1,0:T(8,128)} custom-call(s32[7]{0:T(128)S(1)} %stack.31.place, f32[64,64]{1,0:T(8,128)S(1)} %select_multiply_fusion.table, f32[32,3200]{1,0:T(8,128)S(1)} %get-tuple-element.21.same, f32[32,3200]{1,0:T(8,128)S(1)} %collective-permute-done.other, f32[1,8,3200]{2,1,0:T(8,128)S(1)} %collective-permute-done.4.refs_0_, ...), custom_call_target="tpu_custom_call" | custom-call | tf_op jit(solution)/shard_map/lag_transform/pallas_call | solution.py:261
  (5 shorter events, 0.0 us)
Async XLA Ops:
  0.0 78.8 %copy-start = (s32[32]{0:T(128)S(1)}, s32[32]{0:T(128)}, u32[]{:S(2)}) copy-start(s32[32]{0:T(128)} %param.5) | copy-start | bytes 388
  0.1 1.7 %copy-start.1 = (f32[2,16,80,256]{3,2,1,0:T(8,128)S(1)}, f32[2,16,80,256]{3,2,1,0:T(8,128)}, u32[]{:S(2)}) copy-start(f32[2,16,80,256]{3,2,1,0:T(8,128)} %spectra.9) | copy-start | bytes 7864324
  1.8 0.7 copy-start.2
  3.3 20.3 %collective-permute-start.1 = (f32[2,4,80,256]{3,2,1,0:T(8,128)S(1)}, f32[2,4,80,256]{3,2,1,0:T(8,128)S(1)}, u32[]{:S(2)}, u32[]{:S(2)}) collective-permute-start(f32[2,4,80,256]{3,2,1,0:T(8,128)S(1)} %order_3.1.refs_3_), channel_id=1, source_target_pairs={{0,12},{1,13},{2,14},{3,15},{4,0},{5,1},{6,2},{7,3},{8,4},{9,5},{1... | collective-permute-start | bytes 1966088 | tf_op jit(solution)/shard_map/ppermute | solution.py:295
  9.3 55.2 %collective-permute-start.2 = (f32[2,4,80,256]{3,2,1,0:T(8,128)S(1)}, f32[2,4,80,256]{3,2,1,0:T(8,128)S(1)}, u32[]{:S(2)}, u32[]{:S(2)}) collective-permute-start(f32[2,4,80,256]{3,2,1,0:T(8,128)S(1)} %order_2.1.refs_2_.mine), channel_id=1, source_target_pairs={{0,8},{1,9},{2,10},{3,11},{4,12},{5,13},{6,14},{7,15},{8,0},{9,1},... | collective-permute-start | bytes 1966088 | tf_op jit(solution)/shard_map/ppermute | solution.py:295
  10.3 54.2 %collective-permute-start.3 = (f32[2,4,80,256]{3,2,1,0:T(8,128)S(1)}, f32[2,4,80,256]{3,2,1,0:T(8,128)S(1)}, u32[]{:S(2)}, u32[]{:S(2)}) collective-permute-start(f32[2,4,80,256]{3,2,1,0:T(8,128)S(1)} %order_1.1.refs_1_), channel_id=1, source_target_pairs={{0,4},{1,5},{2,6},{3,7},{4,8},{5,9},{6,10},{7,11},{8,12},{9,13},{1... | collective-permute-start | bytes 1966088 | tf_op jit(solution)/shard_map/ppermute | solution.py:295
  12.2 65.9 %collective-permute-start.15 = (f32[2,4,80,256]{3,2,1,0:T(8,128)S(1)}, f32[2,4,80,256]{3,2,1,0:T(8,128)S(1)}, u32[]{:S(2)}, u32[]{:S(2)}) collective-permute-start(f32[2,4,80,256]{3,2,1,0:T(8,128)S(1)} %order_4.1), channel_id=1, source_target_pairs={{0,4},{1,5},{2,6},{3,7},{4,0},{5,1},{6,2},{7,3},{8,12},{9,13},{10,... | collective-permute-start | bytes 1966088 | tf_op jit(solution)/shard_map/ppermute | solution.py:295
  18.7 62.3 %collective-permute-start = (f32[32,3200]{1,0:T(8,128)S(1)}, f32[32,3200]{1,0:T(8,128)S(1)}, u32[]{:S(2)}, u32[]{:S(2)}) collective-permute-start(f32[32,3200]{1,0:T(8,128)S(1)} %get-tuple-element.22), channel_id=1, source_target_pairs={{0,1},{1,0},{2,3},{3,2},{4,5},{5,4},{6,7},{7,6},{8,9},{9,8},{10,11... | collective-permute-start | bytes 1228808 | tf_op jit(solution)/shard_map/ppermute | solution.py:295
  70.6 0.7 copy-start.3
  71.2 0.7 copy-start.4
  71.9 0.6 copy-start.5
  72.6 0.6 copy-start.6
  73.2 0.6 copy-start.7
  73.8 18.1 %collective-permute-start.4 = (f32[1,8,3200]{2,1,0:T(8,128)}, f32[1,8,3200]{2,1,0:T(8,128)S(1)}, u32[]{:S(2)}, u32[]{:S(2)}) collective-permute-start(f32[1,8,3200]{2,1,0:T(8,128)} %get-tuple-element.23), channel_id=1, source_target_pairs={{0,8},{1,9},{2,10},{3,11},{4,12},{5,13},{6,14},{7,15},{8,0},{9,1},... | collective-permute-start | bytes 307208 | tf_op jit(solution)/shard_map/ppermute | solution.py:295
  77.4 16.2 %collective-permute-start.5 = (f32[1,8,3200]{2,1,0:T(8,128)}, f32[1,8,3200]{2,1,0:T(8,128)S(1)}, u32[]{:S(2)}, u32[]{:S(2)}) collective-permute-start(f32[1,8,3200]{2,1,0:T(8,128)} %get-tuple-element.24), channel_id=1, source_target_pairs={{0,9},{1,8},{2,11},{3,10},{4,13},{5,12},{6,15},{7,14},{8,1},{9,0},... | collective-permute-start | bytes 307208 | tf_op jit(solution)/shard_map/ppermute | solution.py:295
  77.4 17.5 %collective-permute-start.6 = (f32[1,8,3200]{2,1,0:T(8,128)}, f32[1,8,3200]{2,1,0:T(8,128)S(1)}, u32[]{:S(2)}, u32[]{:S(2)}) collective-permute-start(f32[1,8,3200]{2,1,0:T(8,128)} %get-tuple-element.25), channel_id=1, source_target_pairs={{4,12},{5,13},{6,14},{7,15},{12,4},{13,5},{14,6},{15,7},{20,28},{2... | collective-permute-start | bytes 307208 | tf_op jit(solution)/shard_map/ppermute | solution.py:295
  78.1 18.1 %collective-permute-start.7 = (f32[1,8,3200]{2,1,0:T(8,128)}, f32[1,8,3200]{2,1,0:T(8,128)S(1)}, u32[]{:S(2)}, u32[]{:S(2)}) collective-permute-start(f32[1,8,3200]{2,1,0:T(8,128)} %get-tuple-element.26), channel_id=1, source_target_pairs={{4,13},{5,12},{6,15},{7,14},{12,5},{13,4},{14,7},{15,6},{20,29},{2... | collective-permute-start | bytes 307208 | tf_op jit(solution)/shard_map/ppermute | solution.py:295
  81.0 15.4 %collective-permute-start.8 = (f32[1,8,3200]{2,1,0:T(8,128)}, f32[1,8,3200]{2,1,0:T(8,128)S(1)}, u32[]{:S(2)}, u32[]{:S(2)}) collective-permute-start(f32[1,8,3200]{2,1,0:T(8,128)} %copy-done.7), channel_id=1, source_target_pairs={{0,4},{1,5},{2,6},{3,7},{4,8},{5,9},{6,10},{7,11},{8,12},{9,13},{1... | collective-permute-start | bytes 307208 | tf_op jit(solution)/shard_map/ppermute | solution.py:295
  91.9 7.0 %collective-permute-start.9 = (f32[1,8,3200]{2,1,0:T(8,128)}, f32[1,8,3200]{2,1,0:T(8,128)S(1)}, u32[]{:S(2)}, u32[]{:S(2)}) collective-permute-start(f32[1,8,3200]{2,1,0:T(8,128)} %copy-done.6), channel_id=1, source_target_pairs={{0,5},{1,4},{2,7},{3,6},{4,9},{5,8},{6,11},{7,10},{8,13},{9,12},{1... | collective-permute-start | bytes 307208 | tf_op jit(solution)/shard_map/ppermute | solution.py:295
  93.6 9.3 %collective-permute-start.12 = (f32[1,8,3200]{2,1,0:T(8,128)}, f32[1,8,3200]{2,1,0:T(8,128)S(1)}, u32[]{:S(2)}, u32[]{:S(2)}) collective-permute-start(f32[1,8,3200]{2,1,0:T(8,128)} %copy-done.5), channel_id=1, source_target_pairs={{0,4},{1,5},{2,6},{3,7},{8,12},{9,13},{10,14},{11,15},{16,20},{17,... | collective-permute-start | bytes 307208 | tf_op jit(solution)/shard_map/ppermute | solution.py:295
  94.9 8.0 %collective-permute-start.13 = (f32[1,8,3200]{2,1,0:T(8,128)S(1)}, f32[1,8,3200]{2,1,0:T(8,128)S(1)}, u32[]{:S(2)}, u32[]{:S(2)}) collective-permute-start(f32[1,8,3200]{2,1,0:T(8,128)S(1)} %get-tuple-element.32), channel_id=1, source_target_pairs={{0,5},{1,4},{2,7},{3,6},{8,13},{9,12},{10,15},{11,14},{16,21},{17,... | collective-permute-start | bytes 307208 | tf_op jit(solution)/shard_map/ppermute | solution.py:295
  96.2 6.9 %collective-permute-start.16 = (f32[1,8,3200]{2,1,0:T(8,128)S(1)}, f32[1,8,3200]{2,1,0:T(8,128)S(1)}, u32[]{:S(2)}, u32[]{:S(2)}) collective-permute-start(f32[1,8,3200]{2,1,0:T(8,128)S(1)} %get-tuple-element.36), channel_id=1, source_target_pairs={{0,1},{1,0},{2,3},{3,2},{4,5},{5,4},{6,7},{7,6},{8,9},{9,8},{10,11... | collective-permute-start | bytes 307208 | tf_op jit(solution)/shard_map/ppermute | solution.py:295
  96.4 18.1 %collective-permute-start.18 = (f32[1,8,3200]{2,1,0:T(8,128)S(1)}, f32[1,8,3200]{2,1,0:T(8,128)S(1)}, u32[]{:S(2)}, u32[]{:S(2)}) collective-permute-start(f32[1,8,3200]{2,1,0:T(8,128)S(1)} %get-tuple-element.36), channel_id=1, source_target_pairs={{4,1},{5,0},{6,3},{7,2},{12,9},{13,8},{14,11},{15,10},{20,17},{21,... | collective-permute-start | bytes 307208 | tf_op jit(solution)/shard_map/ppermute | solution.py:295
  98.9 15.6 %collective-permute-start.10 = (f32[2,8,3200]{2,1,0:T(8,128)}, f32[2,8,3200]{2,1,0:T(8,128)S(1)}, u32[]{:S(2)}, u32[]{:S(2)}) collective-permute-start(f32[2,8,3200]{2,1,0:T(8,128)} %copy-done.4), channel_id=1, source_target_pairs={{0,12},{1,13},{2,14},{3,15},{4,0},{5,1},{6,2},{7,3},{8,4},{9,5},{1... | collective-permute-start | bytes 614408 | tf_op jit(solution)/shard_map/ppermute | solution.py:295
  102.9 11.6 %collective-permute-start.11 = (f32[2,8,3200]{2,1,0:T(8,128)}, f32[2,8,3200]{2,1,0:T(8,128)S(1)}, u32[]{:S(2)}, u32[]{:S(2)}) collective-permute-start(f32[2,8,3200]{2,1,0:T(8,128)} %copy-done.3), channel_id=1, source_target_pairs={{0,13},{1,12},{2,15},{3,14},{4,1},{5,0},{6,3},{7,2},{8,5},{9,4},{1... | collective-permute-start | bytes 614408 | tf_op jit(solution)/shard_map/ppermute | solution.py:295
  102.9 11.6 %collective-permute-start.14 = (f32[2,8,3200]{2,1,0:T(8,128)S(1)}, f32[2,8,3200]{2,1,0:T(8,128)S(1)}, u32[]{:S(2)}, u32[]{:S(2)}) collective-permute-start(f32[2,8,3200]{2,1,0:T(8,128)S(1)} %get-tuple-element.33), channel_id=1, source_target_pairs={{0,1},{1,0},{2,3},{3,2},{4,5},{5,4},{6,7},{7,6},{8,9},{9,8},{10,11... | collective-permute-start | bytes 614408 | tf_op jit(solution)/shard_map/ppermute | solution.py:295
  103.1 11.4 %collective-permute-start.17 = (f32[1,8,3200]{2,1,0:T(8,128)S(1)}, f32[1,8,3200]{2,1,0:T(8,128)S(1)}, u32[]{:S(2)}, u32[]{:S(2)}) collective-permute-start(f32[1,8,3200]{2,1,0:T(8,128)S(1)} %get-tuple-element.35.refs_12_), channel_id=1, source_target_pairs={{4,0},{5,1},{6,2},{7,3},{12,8},{13,9},{14,10},{15,11},{20,16},{21,... | collective-permute-start | bytes 307208 | tf_op jit(solution)/shard_map/ppermute | solution.py:295

commit v3 on v2

--- a/solution.py
+++ b/solution.py
@@ -284,6 +284,69 @@
     return jnp.where(part[None, :] == 0, jnp.cos(angles), -jnp.sin(angles)) * factor
 
 
+def deliver_kernel(loop_size, moves, *refs):
+    count = len(moves)
+    sources, targets = refs[:count], refs[count : 2 * count]
+    send_sems, recv_sems = refs[2 * count :]
+    quarter = loop_size // MEMBERS
+    chan = lax.axis_index("chan")
+    band = lax.axis_index("band")
+    odd = lax.rem(chan // quarter, 2)
+
+    def device(distance, shift):
+        where = lax.rem(chan + distance * quarter, loop_size)
+        return {"chan": where, "band": lax.rem(band + shift, 2)}
+
+    barrier = pltpu.get_barrier_semaphore()
+    for distance in range(MEMBERS):
+        for shift in range(2):
+            if distance or shift:
+                pl.semaphore_signal(
+                    barrier,
+                    inc=1,
+                    device_id=device(distance, shift),
+                    device_id_type=pl.DeviceIdType.MESH,
+                )
+    pl.semaphore_wait(barrier, 2 * MEMBERS - 1)
+
+    def guarded(parity, action):
+        if parity is None:
+            action()
+        else:
+            pl.when(odd == parity)(action)
+
+    copies = []
+    for at, (distance, shift, parity) in enumerate(moves):
+        copy = pltpu.make_async_remote_copy(
+            src_ref=sources[at],
+            dst_ref=targets[at],
+            send_sem=send_sems.at[at],
+            recv_sem=recv_sems.at[at],
+            device_id=device(distance, shift),
+            device_id_type=pl.DeviceIdType.MESH,
+        )
+        copies.append(copy)
+        guarded(parity, copy.start)
+    for copy, (distance, shift, parity) in zip(copies, moves):
+        guarded(parity, copy.wait_send)
+        guarded(None if parity is None else (parity + distance) % 2, copy.wait_recv)
+
+
+def deliver(loop_size, moves, arrays):
+    count = len(moves)
+    return pl.pallas_call(
+        functools.partial(deliver_kernel, loop_size, moves),
+        out_shape=tuple(jax.ShapeDtypeStruct(array.shape, array.dtype) for array in arrays),
+        in_specs=[VMEM] * count,
+        out_specs=(VMEM,) * count,
+        scratch_shapes=[pltpu.SemaphoreType.DMA((count,)), pltpu.SemaphoreType.DMA((count,))],
+        compiler_params=pltpu.CompilerParams(
+            collective_id=0, has_side_effects=True, vmem_limit_bytes=LIMIT
+        ),
+        name="deliver",
+    )(*arrays)
+
+
 def moved(array, loop_size, distance, shift, wanted):
     quarter = loop_size // MEMBERS
     route = [
@@ -314,22 +377,17 @@
     theirs = moved(swap, loop_size, lambda m: 1 if m % 2 == 0 else -1, 0, every)
     blocks[0] = chunks[0] = ordered_chunk(place, channel_order, spectra, 0)
     same, other = self_pairs(place, chunks)
-    other = moved(other, loop_size, lambda m: 0, 1, every)
     own_same, own_other = extra_pairs(place, chunks[2], theirs)
-    odd = lambda m: m % 2 == 1
-    theirs_same = moved(own_same, loop_size, lambda m: -1, 0, odd)
-    theirs_other = moved(own_other, loop_size, lambda m: -1, 1, odd)
-    own_other = moved(own_other, loop_size, lambda m: 0, 1, every)
     results = partner_pairs(place, blocks)
-    pieces = []
+    moves, arrays = [], []
     for piece, (distance, shift, pairs) in zip(results, PIECES):
-        wanted = every
-        if pairs == (0,):
-            wanted = lambda m: (m + distance) % 2 == 1
         if distance or shift:
-            piece = moved(piece, loop_size, lambda m: distance, shift, wanted)
-        pieces.append(piece)
-    pieces += [own_same, own_other, theirs_same, theirs_other]
+            moves.append((distance, shift, (distance + 1) % 2 if pairs == (0,) else None))
+            arrays.append(piece)
+    moves += [(3, 0, 1), (3, 1, 1), (0, 1, 0), (0, 1, None)]
+    arrays += [own_same, own_other, own_other, other]
+    *pieces, theirs_same, theirs_other, own_other, other = deliver(loop_size, moves, arrays)
+    pieces += [results[-1], own_same, own_other, theirs_same, theirs_other]
     table = lag_table(bin_assign, member, band, 1.0 / spectra.shape[3])
     return lag_transform(place, table, same, other, pieces)[None]
 

time: 118 us -> 106 us (0.90)
  the two profiles are of different devices: /device:TPU:0 before, /device:TPU:31 now
where the time goes in v3:
time: 106 us; the launch traced here: 104 us
  Pallas kernels  48.7 us (46%)
  waiting for transfers between devices  48.5 us (46%)
  starting transfers between devices  3.73 us (4%)
  local copies, waits for them, and re-layouts  3.26 us (3%)
    ppermute x4, waiting for transfers between devices, moved(): return lax.ppermute(array, ('chan', 'band'), route)  48.5 us
    pallas_call x1, Pallas kernels, deliver(): pl.pallas_call(functools.partial(deliver_kernel, loop_size, moves), out_s...  29.6 us
    pallas_call x1, Pallas kernels, partner_pairs(): pl.pallas_call(pair_kernel, out_shape=shapes, in_specs=[SMEM] + [VMEM] *...  6.31 us
    pallas_call x5, Pallas kernels, ordered_chunk(): pl.pallas_call(functools.partial(order_kernel, which), out_shape=jax.Shap...  5.18 us
    ppermute x4, starting transfers between devices, moved(): return lax.ppermute(array, ('chan', 'band'), route)  3.73 us
    pallas_call x1, Pallas kernels, lag_transform(): pl.pallas_call(lag_kernel, out_shape=jax.ShapeDtypeStruct((3, lags, colum...  3.11 us
    pallas_call x1, Pallas kernels, self_pairs(): pl.pallas_call(self_kernel, out_shape=(shape, shape), in_specs=[SMEM] + [...  3.11 us
    unnamed x6, local copies, waits for them, and re-layouts  2.4 us
  transfers between devices with their start and end apart: 4, of which 1 were waited for; matrix products, arithmetic and copies ran while one was open for 1% of the time, Pallas kernels for 8%

profile of v3, /device:TPU:31, one launch (start us, length us, event | category | flops | bytes accessed | tf_op | source)
XLA Modules:
  0.0 104.4 jit_solution(8919935838523786342)
XLA Ops:
  0.0 0.0 copy-start
  0.0 0.1 stack.31.place
  0.1 0.0 copy-start.1
  0.1 1.7 %copy-done.1 = f32[2,16,80,256]{3,2,1,0:T(8,128)S(1)} copy-done((f32[2,16,80,256]{3,2,1,0:T(8,128)S(1)}, f32[2,16,80,256]{3,2,1,0:T(8,128)}, u32[]{:S(2)}) %copy-start.1) | copy-done | bytes 2621464
  1.8 0.0 copy-start.2
  1.8 0.7 copy-done.2
  2.5 0.9 order_3.1.refs_3_
  3.4 0.2 collective-permute-start
  3.6 0.9 order_2.1.refs_2_.mine
  4.4 0.1 collective-permute-start.1
  4.6 0.9 order_1.1.refs_1_
  5.4 3.1 %collective-permute-start.2 = (f32[2,4,80,256]{3,2,1,0:T(8,128)S(1)}, f32[2,4,80,256]{3,2,1,0:T(8,128)}, u32[]{:S(2)}, u32[]{:S(2)}) collective-permute-start(f32[2,4,80,256]{3,2,1,0:T(8,128)S(1)} %order_1.1.refs_1_), channel_id=1, source_target_pairs={{0,4},{1,5},{2,6},{3,7},{4,8},{5,9},{6,10},{7,11},{8,12},{9,13},{1... | collective-permute-start | bytes 1966088 | tf_op jit(solution)/shard_map/ppermute | solution.py:358
  8.5 1.7 %order_4.1 = f32[2,4,80,256]{3,2,1,0:T(8,128)} custom-call(s32[7]{0:T(128)S(1)} %stack.31.place, s32[1,80]{1,0:T(1,128)S(1)} %copy-done.2, f32[2,16,80,256]{3,2,1,0:T(8,128)S(1)} %copy-done.1), custom_call_target="tpu_custom_call" | custom-call | tf_op jit(solution)/shard_map/order_4/pallas_call | solution.py:66
  10.2 0.3 collective-permute-start.3
  10.6 0.9 order_0.1.refs_0_
  11.5 0.0 copy-done
  11.5 0.8 gather_fusion
  12.2 0.2 select_multiply_fusion.table
  12.4 3.1 %self_pairs.1 = (f32[32,3200]{1,0:T(8,128)S(1)}, f32[32,3200]{1,0:T(8,128)S(1)}) custom-call(s32[7]{0:T(128)S(1)} %stack.31.place, f32[2,4,80,256]{3,2,1,0:T(8,128)S(1)} %order_0.1.refs_0_, f32[2,4,80,256]{3,2,1,0:T(8,128)S(1)} %order_1.1.refs_1_, f32[2,4,80,256]{3,2,1,0:T(8,128)S(1)} %order_2.1.refs_2_.mine, f32[2,4,80,256]{3,2,1,0:T(8,128)S(1)} %order_3.1.refs_3_), custom_call_target="tpu_custom_call" | custom-call | flops 5033164800 | bytes 4194304 | tf_op jit(solution)/shard_map/self_pairs/pallas_call | solution.py:181
  15.5 48.5 %collective-permute-done.3.theirs = f32[2,4,80,256]{3,2,1,0:T(8,128)S(1)} collective-permute-done((f32[2,4,80,256]{3,2,1,0:T(8,128)}, f32[2,4,80,256]{3,2,1,0:T(8,128)S(1)}, u32[]{:S(2)}, u32[]{:S(2)}) %collective-permute-start.3) | collective-permute-done | bytes 655392 | tf_op jit(solution)/shard_map/ppermute | solution.py:358
  64.0 1.4 %extra_pairs.1 = (f32[1,8,3200]{2,1,0:T(8,128)S(1)}, f32[1,8,3200]{2,1,0:T(8,128)S(1)}) custom-call(s32[7]{0:T(128)S(1)} %stack.31.place, f32[2,4,80,256]{3,2,1,0:T(8,128)S(1)} %order_2.1.refs_2_.mine, f32[2,4,80,256]{3,2,1,0:T(8,128)S(1)} %collective-permute-done.3.theirs), custom_call_target="tpu_custom_call" | custom-call | tf_op jit(solution)/shard_map/extra_pairs/pallas_call | solution.py:215
  65.4 0.0 collective-permute-done.refs_1_
  65.4 0.0 collective-permute-done.1.refs_2_
  65.4 0.0 collective-permute-done.2.refs_3_
  65.4 6.3 %partner_pairs.1 = (f32[1,8,3200]{2,1,0:T(8,128)S(1)}, f32[1,8,3200]{2,1,0:T(8,128)S(1)}, f32[1,8,3200]{2,1,0:T(8,128)S(1)}, f32[1,8,3200]{2,1,0:T(8,128)S(1)}, ...) custom-call(s32[7]{0:T(128)S(1)} %stack.31.place, ...), custom_call_target="tpu_custom_call" | custom-call | flops 1258291200 | bytes 4194304 | tf_op jit(solution)/shard_map/partner_pairs/pallas_call | solution.py:200
  71.7 29.6 %deliver.1 = (f32[1,8,3200]{2,1,0:T(8,128)S(1)}, f32[1,8,3200]{2,1,0:T(8,128)S(1)}, f32[1,8,3200]{2,1,0:T(8,128)S(1)}, f32[1,8,3200]{2,1,0:T(8,128)S(1)}, f32[1,...) custom-call(f32[1,8,3200]{2,1,0:T(8,128)S(1)} %get-tuple-element.37., ...), custom_call_target="tpu_custom_call" | custom-call | tf_op jit(solution)/shard_map/deliver/pallas_call | solution.py:337
  101.3 3.1 %lag_transform.1 = f32[3,64,3200]{2,1,0:T(8,128)} custom-call(s32[7]{0:T(128)S(1)} %stack.31.place, f32[64,64]{1,0:T(8,128)S(1)} %select_multiply_fusion.table, f32[32,3200]{1,0:T(8,128)S(1)} %get-tuple-element.36.same, f32[32,3200]{1,0:T(8,128)S(1)} %get-tuple-element.51.other, f32[1,8,3200]{2,1,0:T(8,128)S(1)} %get-tuple-element.52.refs_0_, ...), custom_call_target="tpu_custom_call" | custom-call | tf_op jit(solution)/shard_map/lag_transform/pallas_call | solution.py:261
  (3 shorter events, 0.0 us)
Async XLA Ops:
  0.0 11.5 %copy-start = (s32[32]{0:T(128)S(1)}, s32[32]{0:T(128)}, u32[]{:S(2)}) copy-start(s32[32]{0:T(128)} %param.5) | copy-start | bytes 388
  0.1 1.7 %copy-start.1 = (f32[2,16,80,256]{3,2,1,0:T(8,128)S(1)}, f32[2,16,80,256]{3,2,1,0:T(8,128)}, u32[]{:S(2)}) copy-start(f32[2,16,80,256]{3,2,1,0:T(8,128)} %spectra.9) | copy-start | bytes 7864324
  1.8 0.7 copy-start.2
  3.4 62.0 %collective-permute-start = (f32[2,4,80,256]{3,2,1,0:T(8,128)S(1)}, f32[2,4,80,256]{3,2,1,0:T(8,128)}, u32[]{:S(2)}, u32[]{:S(2)}) collective-permute-start(f32[2,4,80,256]{3,2,1,0:T(8,128)S(1)} %order_3.1.refs_3_), channel_id=1, source_target_pairs={{0,12},{1,13},{2,14},{3,15},{4,0},{5,1},{6,2},{7,3},{8,4},{9,5},{1... | collective-permute-start | bytes 1966088 | tf_op jit(solution)/shard_map/ppermute | solution.py:358
  4.4 61.0 %collective-permute-start.1 = (f32[2,4,80,256]{3,2,1,0:T(8,128)S(1)}, f32[2,4,80,256]{3,2,1,0:T(8,128)}, u32[]{:S(2)}, u32[]{:S(2)}) collective-permute-start(f32[2,4,80,256]{3,2,1,0:T(8,128)S(1)} %order_2.1.refs_2_.mine), channel_id=1, source_target_pairs={{0,8},{1,9},{2,10},{3,11},{4,12},{5,13},{6,14},{7,15},{8,0},{9,1},... | collective-permute-start | bytes 1966088 | tf_op jit(solution)/shard_map/ppermute | solution.py:358
  5.4 60.0 %collective-permute-start.2 = (f32[2,4,80,256]{3,2,1,0:T(8,128)S(1)}, f32[2,4,80,256]{3,2,1,0:T(8,128)}, u32[]{:S(2)}, u32[]{:S(2)}) collective-permute-start(f32[2,4,80,256]{3,2,1,0:T(8,128)S(1)} %order_1.1.refs_1_), channel_id=1, source_target_pairs={{0,4},{1,5},{2,6},{3,7},{4,8},{5,9},{6,10},{7,11},{8,12},{9,13},{1... | collective-permute-start | bytes 1966088 | tf_op jit(solution)/shard_map/ppermute | solution.py:358
  10.2 53.7 %collective-permute-start.3 = (f32[2,4,80,256]{3,2,1,0:T(8,128)}, f32[2,4,80,256]{3,2,1,0:T(8,128)S(1)}, u32[]{:S(2)}, u32[]{:S(2)}) collective-permute-start(f32[2,4,80,256]{3,2,1,0:T(8,128)} %order_4.1), channel_id=1, source_target_pairs={{0,4},{1,5},{2,6},{3,7},{4,0},{5,1},{6,2},{7,3},{8,12},{9,13},{10,... | collective-permute-start | bytes 1966088 | tf_op jit(solution)/shard_map/ppermute | solution.py:358

commit v4 on v3

v4 whole, which is shorter than its diff:
```python
import functools
import math

import jax
import jax.numpy as jnp
from jax import lax
from jax.experimental import pallas as pl
from jax.experimental.pallas import tpu as pltpu
from jax.sharding import PartitionSpec as P

MEMBERS = 4
F32 = jnp.float32
BF16 = jnp.bfloat16
VMEM = pl.BlockSpec(memory_space=pltpu.VMEM)
SMEM = pl.BlockSpec(memory_space=pltpu.SMEM)
PIECES = [
    (2, 0, (1,)),
    (2, 1, (1,)),
    (2, 0, (0,)),
    (2, 1, (0,)),
    (1, 0, (1,)),
    (1, 1, (1,)),
    (3, 0, (0, 1)),
    (3, 1, (0, 1)),
    (1, 0, (0,)),
    (1, 1, (0,)),
    (0, 1, (0, 1)),
    (0, 0, (0, 1)),
]
LIMIT = 40 * 1024 * 1024


def halves(x):
    high = x.astype(BF16)
    low = (x - high.astype(F32)).astype(BF16)
    return high, low


def thirds(x):
    high = x.astype(BF16)
    rest = x - high.astype(F32)
    middle = rest.astype(BF16)
    low = (rest - middle.astype(F32)).astype(BF16)
    return high, middle, low


def dot(left, right, dims):
    return lax.dot_general(left, right, (dims, ((), ())), preferred_element_type=F32)


def ordered_rows(chosen, values):
    stacked = jnp.concatenate(thirds(values), axis=0)
    return dot(chosen, stacked, ((0,), (0,)))


def left_operand(real, imag):
    stacked = jnp.concatenate(
        [
            jnp.concatenate([real, imag], axis=1),
            jnp.concatenate([imag, -real], axis=1),
        ],
        axis=0,
    )
    return halves(stacked)


def right_operand(real, imag):
    return halves(jnp.concatenate([real, imag], axis=1))


def product(left, right):
    dims = ((1,), (1,))
    return (
        dot(left[0], right[0], dims)
        + dot(left[0], right[1], dims)
        + dot(left[1], right[0], dims)
    )


def packed_rows(scratch, lead, first, rows, group, count):
    pieces = [
        scratch[lead, pl.ds(first + group * 8 + step, count, stride=rows), :][:, :rows]
        for step in range(8)
    ]
    return jnp.concatenate(pieces, axis=1)


def put_product(scratch, lead, slot, value):
    rows = value.shape[1]
    scratch[lead, slot * 2 * rows : (slot + 1) * 2 * rows, 0:rows] = value


def exchange_kernel(loop_size, moves, order, spectra, *refs):
    count = len(moves)
    same, own_same, kept = refs[:3]
    targets = refs[3 : 3 + count]
    sources = refs[3 + count : 3 + 2 * count]
    chunks, blocks, scratch, send_sems, recv_sems, go_sems, come_sems = refs[3 + 2 * count :]
    _, bins, _, rows, _ = chunks.shape
    half = rows // 2
    packed = 2 * bins
    width = 8 * rows
    quarter = loop_size // MEMBERS
    chan = lax.axis_index("chan")
    band = lax.axis_index("band")
    member = chan // quarter
    parity = lax.rem(member, 2)
    even = parity == 0
    swap = 1 - 2 * parity

    def device(distance, shift):
        where = lax.rem(chan + distance * quarter + loop_size, loop_size)
        return {"chan": where, "band": lax.rem(band + shift, 2)}

    def send(source, target, send_sem, recv_sem, where):
        return pltpu.make_async_remote_copy(
            src_ref=source,
            dst_ref=target,
            send_sem=send_sem,
            recv_sem=recv_sem,
            device_id=where,
            device_id_type=pl.DeviceIdType.MESH,
        )

    barrier = pltpu.get_barrier_semaphore()
    for distance in range(MEMBERS):
        for shift in range(2):
            if distance or shift:
                pl.semaphore_signal(
                    barrier,
                    inc=1,
                    device_id=device(distance, shift),
                    device_id_type=pl.DeviceIdType.MESH,
                )

    row_ids = lax.broadcasted_iota(jnp.int32, (rows, rows), 0)
    chosen = jnp.where(row_ids == order[...], 1.0, 0.0).astype(BF16)
    chosen = jnp.concatenate([chosen] * 3, axis=0)

    def arrange(which, slot):
        if which == MEMBERS:
            chunk = lax.rem(member + 3 - 2 * parity, MEMBERS)
        else:
            chunk = lax.rem(member + which, MEMBERS)
        for part in range(2):
            values = spectra[part, chunk * bins + slot]
            chunks[which, slot, part] = ordered_rows(chosen, values)

    forward = {}
    for slot in range(bins):
        for which in (2, 3, 1, MEMBERS):
            arrange(which, slot)
            landing = 0 if which == MEMBERS else MEMBERS - which
            at = slot * MEMBERS + landing
            forward[slot, landing] = send(
                chunks.at[which, slot],
                blocks.at[landing, slot],
                go_sems.at[at],
                come_sems.at[at],
                device(swap if which == MEMBERS else which, 0),
            )
        if slot == 0:
            pl.semaphore_wait(barrier, 2 * MEMBERS - 1)
        for landing in (2, 1, 3, 0):
            forward[slot, landing].start()

    def guarded(wanted, action):
        if wanted is None:
            action()
        else:
            pl.when(parity == wanted)(action)

    def start(at):
        distance, shift, wanted = moves[at]
        copy = send(
            sources[at], targets[at], send_sems.at[at], recv_sems.at[at], device(distance, shift)
        )
        guarded(wanted, copy.start)
        return copy

    def fill(out, row, lead, shift):
        first = lax.rem(band + shift, 2) * half
        for group in range(half // 8):
            out[row, :, group * width : (group + 1) * width] = (
                packed_rows(scratch, lead, first, rows, group, packed)
            )

    returns = [None] * count
    for distance in range(MEMBERS):
        for slot in range(bins):
            if distance == 0:
                arrange(0, slot)
            real, imag = chunks[distance, slot, 0], chunks[distance, slot, 1]
            put_product(
                scratch,
                2 * MEMBERS + 1 + distance,
                slot,
                product(left_operand(real, imag), right_operand(real, imag)),
            )
        block = (MEMBERS - distance) % MEMBERS
        fill(same, block, 2 * MEMBERS + 1 + distance, 0)
        fill(sources[count - 1], block, 2 * MEMBERS + 1 + distance, 1)
    returns[count - 1] = start(count - 1)

    for slot in range(bins):
        for landing in (2, 1, 3, 0):
            forward[slot, landing].wait_recv()
        lefts, rights = [], []
        for at in range(MEMBERS):
            block = blocks if at else chunks
            real, imag = block[at, slot, 0], block[at, slot, 1]
            lefts.append(left_operand(real, imag))
            rights.append(right_operand(real, imag))
        for owner in (2, 1, 3, 0):
            for pair in range(2):
                partner = (owner + pair + 1) % MEMBERS
                put_product(scratch, owner * 2 + pair, slot, product(lefts[owner], rights[partner]))
        mine = [chunks[2, slot, part] for part in range(2)]
        theirs = [blocks[0, slot, part] for part in range(2)]
        first = [jnp.where(even, a, b) for a, b in zip(mine, theirs)]
        second = [jnp.where(even, b, a) for a, b in zip(mine, theirs)]
        put_product(
            scratch, 2 * MEMBERS, slot, product(left_operand(*first), right_operand(*second))
        )

    for at, (owner, shift, pairs) in enumerate(PIECES[:-1]):
        for row, pair in enumerate(pairs):
            fill(sources[at], row, owner * 2 + pair, shift)
        returns[at] = start(at)
    fill(own_same, 0, 2 * MEMBERS, 0)
    base = len(PIECES) - 1
    fill(sources[base], 0, 2 * MEMBERS, 0)
    returns[base] = start(base)
    fill(sources[base + 1], 0, 2 * MEMBERS, 1)
    fill(sources[base + 2], 0, 2 * MEMBERS, 1)
    returns[base + 1] = start(base + 1)
    returns[base + 2] = start(base + 2)
    for row, pair in enumerate(PIECES[-1][2]):
        fill(kept, row, pair, 0)

    for copy in forward.values():
        copy.wait_send()
    for copy, (distance, shift, wanted) in zip(returns, moves):
        guarded(wanted, copy.wait_send)
        guarded(None if wanted is None else (wanted + distance) % 2, copy.wait_recv)


def exchange(loop_size, order, spectra):
    _, bins, rows, windows = spectra.shape
    bins = bins // MEMBERS
    columns = rows * rows // 2
    moves, leads = [], []
    for distance, shift, pairs in PIECES[:-1]:
        moves.append((distance, shift, (distance + 1) % 2 if pairs == (0,) else None))
        leads.append(len(pairs))
    moves += [(3, 0, 1), (3, 1, 1), (0, 1, 0), (0, 1, None)]
    leads += [1, 1, 1, MEMBERS]
    count = len(moves)
    outs = [(lead, 2 * bins, columns) for lead in [MEMBERS, 1, 2] + leads]
    results = pl.pallas_call(
        functools.partial(exchange_kernel, loop_size, moves),
        out_shape=tuple(jax.ShapeDtypeStruct(shape, F32) for shape in outs),
        in_specs=[VMEM, VMEM],
        out_specs=(VMEM,) * len(outs),
        scratch_shapes=[pltpu.VMEM((lead, 2 * bins, columns), F32) for lead in leads]
        + [
            pltpu.VMEM((MEMBERS + 1, bins, 2, rows, windows), F32),
            pltpu.VMEM((MEMBERS, bins, 2, rows, windows), F32),
            pltpu.VMEM((3 * MEMBERS + 1, 2 * bins * rows, 128), F32),
            pltpu.SemaphoreType.DMA((count,)),
            pltpu.SemaphoreType.DMA((count,)),
            pltpu.SemaphoreType.DMA((bins * MEMBERS,)),
            pltpu.SemaphoreType.DMA((bins * MEMBERS,)),
        ],
        compiler_params=pltpu.CompilerParams(
            collective_id=0, has_side_effects=True, vmem_limit_bytes=LIMIT
        ),
        name="exchange",
    )(order, spectra)
    return results[:3], results[3:]


def lag_kernel(place, table, same, other, *refs):
    pieces, extras, out = refs[: len(PIECES)], refs[len(PIECES) : -1], refs[-1]
    columns = out.shape[2]
    tile = 640 if columns % 640 == 0 else columns
    high, low = halves(table[...])
    dims = ((1,), (0,))
    even = lax.rem(place[0], 2) == 0
    found = {}
    for piece, (distance, shift, pairs) in zip(pieces, PIECES):
        for row, pair in enumerate(pairs):
            found[pair, shift, distance] = piece, row
    own_same, own_other, theirs_same, theirs_other = extras
    more = {(1, 0): theirs_same, (1, 1): theirs_other, (2, 0): own_same, (2, 1): own_other}
    for pair in range(3):
        for at in range(0, columns, tile):
            span = slice(at, at + tile)
            if pair == 0:
                stacked = jnp.concatenate([same[:, span], other[:, span]], axis=0)
            else:
                terms = []
                for shift in range(2):
                    for distance in range(MEMBERS):
                        piece, row = found[pair - 1, shift, distance]
                        term = piece[row, :, span]
                        if pair == 1 and (distance, shift) in more:
                            term = jnp.where(even, more[distance, shift][0, :, span], term)
                        terms.append(term)
                stacked = jnp.concatenate(terms, axis=0)
            first, second = halves(stacked)
            out[pair, :, span] = dot(high, first, dims) + dot(high, second, dims) + dot(low, first, dims)


def lag_transform(place, table, same, other, pieces):
    lags = table.shape[0]
    columns = same.shape[1]
    return pl.pallas_call(
        lag_kernel,
        out_shape=jax.ShapeDtypeStruct((3, lags, columns), F32),
        in_specs=[SMEM] + [VMEM] * (3 + len(pieces)),
        out_specs=VMEM,
        compiler_params=pltpu.CompilerParams(vmem_limit_bytes=LIMIT),
        name="lag_transform",
    )(place, table, same, other, *pieces)


def lag_table(bin_assign, member, band, factor):
    bins = bin_assign.shape[0]
    lags = 2 * bins
    chunk = bins // (2 * MEMBERS)
    column = jnp.arange(lags, dtype=jnp.int32)
    shift = column // (MEMBERS * 2 * chunk)
    distance = column // (2 * chunk) % MEMBERS
    slot = column // 2 % chunk
    part = column % 2
    where = (band + shift) % 2 * (MEMBERS * chunk) + (member - distance + MEMBERS) % MEMBERS * chunk + slot
    steps = jnp.arange(lags, dtype=jnp.int32)
    phase = steps[:, None] * bin_assign[where][None, :] % lags
    angles = phase.astype(F32) * (2.0 * math.pi / lags)
    return jnp.where(part[None, :] == 0, jnp.cos(angles), -jnp.sin(angles)) * factor


def deliver_kernel(loop_size, moves, *refs):
    count = len(moves)
    sources, targets = refs[:count], refs[count : 2 * count]
    send_sems, recv_sems = refs[2 * count :]
    quarter = loop_size // MEMBERS
    chan = lax.axis_index("chan")
    band = lax.axis_index("band")
    odd = lax.rem(chan // quarter, 2)

    def device(distance, shift):
        where = lax.rem(chan + distance * quarter, loop_size)
        return {"chan": where, "band": lax.rem(band + shift, 2)}

    barrier = pltpu.get_barrier_semaphore()
    for distance in range(MEMBERS):
        for shift in range(2):
            if distance or shift:
                pl.semaphore_signal(
                    barrier,
                    inc=1,
                    device_id=device(distance, shift),
                    device_id_type=pl.DeviceIdType.MESH,
                )
    pl.semaphore_wait(barrier, 2 * MEMBERS - 1)

    def guarded(parity, action):
        if parity is None:
            action()
        else:
            pl.when(odd == parity)(action)

    copies = []
    for at, (distance, shift, parity) in enumerate(moves):
        copy = pltpu.make_async_remote_copy(
            src_ref=sources[at],
            dst_ref=targets[at],
            send_sem=send_sems.at[at],
            recv_sem=recv_sems.at[at],
            device_id=device(distance, shift),
            device_id_type=pl.DeviceIdType.MESH,
        )
        copies.append(copy)
        guarded(parity, copy.start)
    for copy, (distance, shift, parity) in zip(copies, moves):
        guarded(parity, copy.wait_send)
        guarded(None if parity is None else (parity + distance) % 2, copy.wait_recv)


def deliver(loop_size, moves, arrays):
    count = len(moves)
    return pl.pallas_call(
        functools.partial(deliver_kernel, loop_size, moves),
        out_shape=tuple(jax.ShapeDtypeStruct(array.shape, array.dtype) for array in arrays),
        in_specs=[VMEM] * count,
        out_specs=(VMEM,) * count,
        scratch_shapes=[pltpu.SemaphoreType.DMA((count,)), pltpu.SemaphoreType.DMA((count,))],
        compiler_params=pltpu.CompilerParams(
            collective_id=0, has_side_effects=True, vmem_limit_bytes=LIMIT
        ),
        name="deliver",
    )(*arrays)


def on_device(loop_size, spectra, channel_order, bin_assign):
    member = lax.axis_index("chan") // (loop_size // MEMBERS)
    band = lax.axis_index("band")
    place = jnp.stack([member, band]).astype(jnp.int32)
    local, returned = exchange(loop_size, channel_order, spectra)
    same, own_same, kept = local
    *pieces, theirs_same, theirs_other, own_other, other = returned
    pieces += [kept, own_same, own_other, theirs_same, theirs_other]
    table = lag_table(bin_assign, member, band, 1.0 / spectra.shape[3])
    flat = (MEMBERS * same.shape[1], same.shape[2])
    return lag_transform(place, table, same.reshape(flat), other.reshape(flat), pieces)[None]


def solution(mesh):
    in_specs = (P(None, "band", ("grp", "chan"), None), P(("grp", "chan"), None), P())
    out_specs = P(("grp", "chan"), None, None, "band")
    return jax.shard_map(
        functools.partial(on_device, mesh.shape["chan"]),
        mesh=mesh,
        in_specs=in_specs,
        out_specs=out_specs,
        check_vma=False,
    )
```

time: 106 us -> 98.2 us (0.926)
  waiting for transfers between devices: 48.5 us -> 0 us
  Pallas kernels: 48.7 us -> 93.3 us
  starting transfers between devices: 3.73 us -> 0 us
    ppermute x4 -> x0, waiting for transfers between devices: 48.5 us -> none  [moved(): return lax.ppermute(array, ('chan', 'band'), route)]
    pallas_call x9 -> x1, Pallas kernels: 45.6 us -> 90.1 us  [exchange(): pl.pallas_call(functools.partial(exchange_kernel, loop_size, moves), out_...]
    ppermute x4 -> x0, starting transfers between devices: 3.73 us -> none  [moved(): return lax.ppermute(array, ('chan', 'band'), route)]
  transfers between devices with their start and end apart: 4 -> 0, of which waited for: 1 -> 0; matrix products, arithmetic and copies ran while one was open for 1% -> 0% of each run, Pallas kernels for 8% -> 0%
where the time goes in v4:
time: 98.2 us; the launch traced here: 97.3 us
  Pallas kernels  93.3 us (95%)
  local copies, waits for them, and re-layouts  3.69 us (4%)
    pallas_call x1, Pallas kernels, exchange(): pl.pallas_call(functools.partial(exchange_kernel, loop_size, moves), out_...  90.1 us
    pallas_call x1, Pallas kernels, lag_transform(): pl.pallas_call(lag_kernel, out_shape=jax.ShapeDtypeStruct((3, lags, colum...  3.12 us
    unnamed x6, local copies, waits for them, and re-layouts  2.92 us

profile of v4, /device:TPU:31, one launch (start us, length us, event | category | flops | bytes accessed | tf_op | source)
XLA Modules:
  0.0 97.3 jit_solution(11776681464397538791)
XLA Ops:
  0.0 0.0 copy-start
  0.0 0.1 pad_add_fusion.place
  0.1 0.5 copy-done
  0.7 0.8 gather_fusion
  1.4 0.2 select_multiply_fusion.table
  1.6 0.0 copy-start.1
  1.6 1.7 %copy-done.1 = f32[2,16,80,256]{3,2,1,0:T(8,128)S(1)} copy-done((f32[2,16,80,256]{3,2,1,0:T(8,128)S(1)}, f32[2,16,80,256]{3,2,1,0:T(8,128)}, u32[]{:S(2)}) %copy-start.1) | copy-done | bytes 2621464
  3.3 0.0 copy-start.2
  3.3 0.7 copy-done.2
  4.0 90.1 %exchange.1 = (f32[4,8,3200]{2,1,0:T(8,128)S(1)}, f32[1,8,3200]{2,1,0:T(8,128)S(1)}, f32[2,8,3200]{2,1,0:T(8,128)S(1)}, f32[1,8,3200]{2,1,0:T(8,128)S(1)}, f32[1...) custom-call(s32[1,80]{1,0:T(1,128)S(1)} %copy-done.2, ...), custom_call_target="tpu_custom_call" | custom-call | tf_op jit(solution)/shard_map/exchange/pallas_call | solution.py:260
  94.1 3.1 %lag_transform.1 = f32[3,64,3200]{2,1,0:T(8,128)} custom-call(s32[2]{0:T(128)S(1)} %pad_add_fusion.place, f32[64,64]{1,0:T(8,128)S(1)} %select_multiply_fusion.table, f32[32,3200]{1,0:T(8,128)S(1)} %bitcast.7, f32[32,3200]{1,0:T(8,128)S(1)} %bitcast.8, f32[1,8,3200]{2,1,0:T(8,128)S(1)} %get-tuple-element.25.refs_0_, ...), custom_call_target="tpu_custom_call" | custom-call | tf_op jit(solution)/shard_map/lag_transform/pallas_call | solution.py:318
  (3 shorter events, 0.0 us)
Async XLA Ops:
  0.0 0.7 copy-start
  1.6 1.7 %copy-start.1 = (f32[2,16,80,256]{3,2,1,0:T(8,128)S(1)}, f32[2,16,80,256]{3,2,1,0:T(8,128)}, u32[]{:S(2)}) copy-start(f32[2,16,80,256]{3,2,1,0:T(8,128)} %spectra.1) | copy-start | bytes 7864324
  3.3 0.7 copy-start.2

commit v5 on v4

--- a/solution.py
+++ b/solution.py
@@ -12,6 +12,7 @@
 F32 = jnp.float32
 BF16 = jnp.bfloat16
 VMEM = pl.BlockSpec(memory_space=pltpu.VMEM)
+HBM = pl.BlockSpec(memory_space=pltpu.HBM)
 SMEM = pl.BlockSpec(memory_space=pltpu.SMEM)
 PIECES = [
     (2, 0, (1,)),
@@ -90,12 +91,45 @@
     scratch[lead, slot * 2 * rows : (slot + 1) * 2 * rows, 0:rows] = value
 
 
-def exchange_kernel(loop_size, moves, order, spectra, *refs):
+def lag_table(assign, member, band, bins, factor):
+    total = assign.shape[1]
+    lags = 2 * total
+    column = lax.broadcasted_iota(jnp.int32, (total, lags), 1)
+    shift = lax.div(column, MEMBERS * 2 * bins)
+    distance = lax.rem(lax.div(column, 2 * bins), MEMBERS)
+    slot = lax.rem(lax.div(column, 2), bins)
+    chunk = lax.rem(member - distance + MEMBERS, MEMBERS)
+    where = lax.rem(band + shift, 2) * (MEMBERS * bins) + chunk * bins + slot
+    chosen = lax.broadcasted_iota(jnp.int32, (total, lags), 0) == where
+    chosen = jnp.where(chosen, 1.0, 0.0).astype(BF16)
+    many = jnp.broadcast_to(assign, (16, total)).astype(F32).astype(BF16)
+    held = dot(many, chosen, ((1,), (0,)))[0:1, :]
+    steps = lax.broadcasted_iota(jnp.int32, (lags, lags), 0).astype(F32)
+    phase = steps * held
+    phase = phase - jnp.floor(phase * (1.0 / lags)) * lags
+    angles = phase * (2.0 * math.pi / lags)
+    part = lax.rem(lax.broadcasted_iota(jnp.int32, (lags, lags), 1), 2)
+    return jnp.where(part == 0, jnp.cos(angles), -jnp.sin(angles)) * factor
+
+
+def exchange_kernel(loop_size, moves, order_hbm, spectra_hbm, assign_hbm, *refs):
     count = len(moves)
-    same, own_same, kept = refs[:3]
-    targets = refs[3 : 3 + count]
-    sources = refs[3 + count : 3 + 2 * count]
-    chunks, blocks, scratch, send_sems, recv_sems, go_sems, come_sems = refs[3 + 2 * count :]
+    same, own_same, kept, table = refs[:4]
+    targets = refs[4 : 4 + count]
+    sources = refs[4 + count : 4 + 2 * count]
+    (
+        order,
+        spectra,
+        assign,
+        chunks,
+        blocks,
+        scratch,
+        send_sems,
+        recv_sems,
+        go_sems,
+        come_sems,
+        in_sems,
+    ) = refs[4 + 2 * count :]
     _, bins, _, rows, _ = chunks.shape
     half = rows // 2
     packed = 2 * bins
@@ -132,6 +166,17 @@
                     device_id=device(distance, shift),
                     device_id_type=pl.DeviceIdType.MESH,
                 )
+
+    fetches = [
+        pltpu.make_async_copy(order_hbm, order, in_sems.at[0]),
+        pltpu.make_async_copy(spectra_hbm.at[0], spectra.at[0], in_sems.at[1]),
+        pltpu.make_async_copy(spectra_hbm.at[1], spectra.at[1], in_sems.at[2]),
+        pltpu.make_async_copy(assign_hbm, assign, in_sems.at[3]),
+    ]
+    for fetch in fetches:
+        fetch.start()
+    for fetch in fetches:
+        fetch.wait()
 
     row_ids = lax.broadcasted_iota(jnp.int32, (rows, rows), 0)
     chosen = jnp.where(row_ids == order[...], 1.0, 0.0).astype(BF16)
@@ -185,6 +230,7 @@
                 packed_rows(scratch, lead, first, rows, group, packed)
             )
 
+    table[...] = lag_table(assign[...], member, band, bins, 1.0 / spectra.shape[3])
     returns = [None] * count
     for distance in range(MEMBERS):
         for slot in range(bins):
@@ -245,7 +291,7 @@
         guarded(None if wanted is None else (wanted + distance) % 2, copy.wait_recv)
 
 
-def exchange(loop_size, order, spectra):
+def exchange(loop_size, order, spectra, assign):
     _, bins, rows, windows = spectra.shape
     bins = bins // MEMBERS
     columns = rows * rows // 2
@@ -257,13 +303,17 @@
     leads += [1, 1, 1, MEMBERS]
     count = len(moves)
     outs = [(lead, 2 * bins, columns) for lead in [MEMBERS, 1, 2] + leads]
+    outs.insert(3, (4 * MEMBERS * bins, 4 * MEMBERS * bins))
     results = pl.pallas_call(
         functools.partial(exchange_kernel, loop_size, moves),
         out_shape=tuple(jax.ShapeDtypeStruct(shape, F32) for shape in outs),
-        in_specs=[VMEM, VMEM],
+        in_specs=[HBM, HBM, HBM],
         out_specs=(VMEM,) * len(outs),
         scratch_shapes=[pltpu.VMEM((lead, 2 * bins, columns), F32) for lead in leads]
         + [
+            pltpu.VMEM(order.shape, jnp.int32),
+            pltpu.VMEM(spectra.shape, F32),
+            pltpu.VMEM(assign.shape, jnp.int32),
             pltpu.VMEM((MEMBERS + 1, bins, 2, rows, windows), F32),
             pltpu.VMEM((MEMBERS, bins, 2, rows, windows), F32),
             pltpu.VMEM((3 * MEMBERS + 1, 2 * bins * rows, 128), F32),
@@ -271,17 +321,19 @@
             pltpu.SemaphoreType.DMA((count,)),
             pltpu.SemaphoreType.DMA((bins * MEMBERS,)),
             pltpu.SemaphoreType.DMA((bins * MEMBERS,)),
+            pltpu.SemaphoreType.DMA((4,)),
         ],
         compiler_params=pltpu.CompilerParams(
-            collective_id=0, has_side_effects=True, vmem_limit_bytes=LIMIT
+            collective_id=0, has_side_effects=True, vmem_limit_bytes=50 * 1024 * 1024
         ),
         name="exchange",
-    )(order, spectra)
-    return results[:3], results[3:]
+    )(order, spectra, assign)
+    return results[:4], results[4:]
 
 
 def lag_kernel(place, table, same, other, *refs):
-    pieces, extras, out = refs[: len(PIECES)], refs[len(PIECES) : -1], refs[-1]
+    pieces, extras, written = refs[: len(PIECES)], refs[len(PIECES) : -3], refs[-3]
+    out, sems = refs[-2:]
     columns = out.shape[2]
     tile = 640 if columns % 640 == 0 else columns
     high, low = halves(table[...])
@@ -293,6 +345,7 @@
             found[pair, shift, distance] = piece, row
     own_same, own_other, theirs_same, theirs_other = extras
     more = {(1, 0): theirs_same, (1, 1): theirs_other, (2, 0): own_same, (2, 1): own_other}
+    writes = []
     for pair in range(3):
         for at in range(0, columns, tile):
             span = slice(at, at + tile)
@@ -310,6 +363,11 @@
                 stacked = jnp.concatenate(terms, axis=0)
             first, second = halves(stacked)
             out[pair, :, span] = dot(high, first, dims) + dot(high, second, dims) + dot(low, first, dims)
+        write = pltpu.make_async_copy(out.at[pair], written.at[pair], sems.at[pair])
+        write.start()
+        writes.append(write)
+    for write in writes:
+        write.wait()
 
 
 def lag_transform(place, table, same, other, pieces):
@@ -319,100 +377,21 @@
         lag_kernel,
         out_shape=jax.ShapeDtypeStruct((3, lags, columns), F32),
         in_specs=[SMEM] + [VMEM] * (3 + len(pieces)),
-        out_specs=VMEM,
+        out_specs=HBM,
+        scratch_shapes=[pltpu.VMEM((3, lags, columns), F32), pltpu.SemaphoreType.DMA((3,))],
         compiler_params=pltpu.CompilerParams(vmem_limit_bytes=LIMIT),
         name="lag_transform",
     )(place, table, same, other, *pieces)
-
-
-def lag_table(bin_assign, member, band, factor):
-    bins = bin_assign.shape[0]
-    lags = 2 * bins
-    chunk = bins // (2 * MEMBERS)
-    column = jnp.arange(lags, dtype=jnp.int32)
-    shift = column // (MEMBERS * 2 * chunk)
-    distance = column // (2 * chunk) % MEMBERS
-    slot = column // 2 % chunk
-    part = column % 2
-    where = (band + shift) % 2 * (MEMBERS * chunk) + (member - distance + MEMBERS) % MEMBERS * chunk + slot
-    steps = jnp.arange(lags, dtype=jnp.int32)
-    phase = steps[:, None] * bin_assign[where][None, :] % lags
-    angles = phase.astype(F32) * (2.0 * math.pi / lags)
-    return jnp.where(part[None, :] == 0, jnp.cos(angles), -jnp.sin(angles)) * factor
-
-
-def deliver_kernel(loop_size, moves, *refs):
-    count = len(moves)
-    sources, targets = refs[:count], refs[count : 2 * count]
-    send_sems, recv_sems = refs[2 * count :]
-    quarter = loop_size // MEMBERS
-    chan = lax.axis_index("chan")
-    band = lax.axis_index("band")
-    odd = lax.rem(chan // quarter, 2)
-
-    def device(distance, shift):
-        where = lax.rem(chan + distance * quarter, loop_size)
-        return {"chan": where, "band": lax.rem(band + shift, 2)}
-
-    barrier = pltpu.get_barrier_semaphore()
-    for distance in range(MEMBERS):
-        for shift in range(2):
-            if distance or shift:
-                pl.semaphore_signal(
-                    barrier,
-                    inc=1,
-                    device_id=device(distance, shift),
-                    device_id_type=pl.DeviceIdType.MESH,
-                )
-    pl.semaphore_wait(barrier, 2 * MEMBERS - 1)
-
-    def guarded(parity, action):
-        if parity is None:
-            action()
-        else:
-            pl.when(odd == parity)(action)
-
-    copies = []
-    for at, (distance, shift, parity) in enumerate(moves):
-        copy = pltpu.make_async_remote_copy(
-            src_ref=sources[at],
-            dst_ref=targets[at],
-            send_sem=send_sems.at[at],
-            recv_sem=recv_sems.at[at],
-            device_id=device(distance, shift),
-            device_id_type=pl.DeviceIdType.MESH,
-        )
-        copies.append(copy)
-        guarded(parity, copy.start)
-    for copy, (distance, shift, parity) in zip(copies, moves):
-        guarded(parity, copy.wait_send)
-        guarded(None if parity is None else (parity + distance) % 2, copy.wait_recv)
-
-
-def deliver(loop_size, moves, arrays):
-    count = len(moves)
-    return pl.pallas_call(
-        functools.partial(deliver_kernel, loop_size, moves),
-        out_shape=tuple(jax.ShapeDtypeStruct(array.shape, array.dtype) for array in arrays),
-        in_specs=[VMEM] * count,
-        out_specs=(VMEM,) * count,
-        scratch_shapes=[pltpu.SemaphoreType.DMA((count,)), pltpu.SemaphoreType.DMA((count,))],
-        compiler_params=pltpu.CompilerParams(
-            collective_id=0, has_side_effects=True, vmem_limit_bytes=LIMIT
-        ),
-        name="deliver",
-    )(*arrays)
 
 
 def on_device(loop_size, spectra, channel_order, bin_assign):
     member = lax.axis_index("chan") // (loop_size // MEMBERS)
     band = lax.axis_index("band")
     place = jnp.stack([member, band]).astype(jnp.int32)
-    local, returned = exchange(loop_size, channel_order, spectra)
-    same, own_same, kept = local
+    local, returned = exchange(loop_size, channel_order, spectra, bin_assign[None, :])
+    same, own_same, kept, table = local
     *pieces, theirs_same, theirs_other, own_other, other = returned
     pieces += [kept, own_same, own_other, theirs_same, theirs_other]
-    table = lag_table(bin_assign, member, band, 1.0 / spectra.shape[3])
     flat = (MEMBERS * same.shape[1], same.shape[2])
     return lag_transform(place, table, same.reshape(flat), other.reshape(flat), pieces)[None]
 

time: 98.2 us -> 95.2 us (0.969)
  local copies, waits for them, and re-layouts: 3.69 us -> 1.31 us
    unnamed x6 -> x4, local copies, waits for them, and re-layouts: 2.92 us -> 1.31 us
where the time goes in v5:
time: 95.2 us; the launch traced here: 94.2 us
  Pallas kernels  92.8 us (97%)
  local copies, waits for them, and re-layouts  1.31 us (1%)
    pallas_call x1, Pallas kernels, exchange(): pl.pallas_call(functools.partial(exchange_kernel, loop_size, moves), out_...  90.2 us
    pallas_call x1, Pallas kernels, lag_transform(): pl.pallas_call(lag_kernel, out_shape=jax.ShapeDtypeStruct((3, lags, colum...  2.6 us

profile of v5, /device:TPU:31, one launch (start us, length us, event | category | flops | bytes accessed | tf_op | source)
XLA Modules:
  0.0 94.2 jit_solution(6805306542413367495)
XLA Ops:
  0.0 0.1 pad_add_fusion.place
  0.1 0.0 copy-start
  0.1 0.7 copy-done
  0.7 0.0 copy-start.1
  0.7 0.7 copy-done.1
  1.4 90.2 %exchange.1 = (f32[4,8,3200]{2,1,0:T(8,128)S(1)}, f32[1,8,3200]{2,1,0:T(8,128)S(1)}, f32[2,8,3200]{2,1,0:T(8,128)S(1)}, f32[64,64]{1,0:T(8,128)S(1)}, f32[1,8,32...) custom-call(s32[1,80]{1,0:T(1,128)S(1)} %copy-done, ...), custom_call_target="tpu_custom_call" | custom-call | tf_op jit(solution)/shard_map/exchange/pallas_call | solution.py:307
  91.6 2.6 %lag_transform.1 = f32[3,64,3200]{2,1,0:T(8,128)} custom-call(s32[2]{0:T(128)S(1)} %pad_add_fusion.place, f32[64,64]{1,0:T(8,128)S(1)} %get-tuple-element.24.table, f32[32,3200]{1,0:T(8,128)S(1)} %bitcast.6, f32[32,3200]{1,0:T(8,128)S(1)} %bitcast.7, f32[1,8,3200]{2,1,0:T(8,128)S(1)} %get-tuple-element.27.refs_0_, ...), custom_call_target="tpu_custom_call" | custom-call | tf_op jit(solution)/shard_map/lag_transform/pallas_call | solution.py:376
Async XLA Ops:
  0.1 0.7 copy-start
  0.7 0.7 copy-start.1
